TPU v7x, 128 devices: a whole 4x4x4 slice. The times are simulated.
128 devices in a mesh: wide: 16 (over y, x), narrow: 8 (over z, core).
Axes of the slice: x: 4, y: 4, z: 4, core: 2. Of those that a mesh axis runs over, the one named last changes fastest.
Arguments:
- initial: float32 [2, 512, 256, 128], P(None, 'wide', 'narrow'), may hold values from 0.5 to 2
- images: float32 [2, 4, 48, 48, 128], P(None, None, 'wide', 'narrow'), may hold values from 20 to 200
- blocks: bfloat16 [4, 8, 128, 128], replicated, may hold values from 0 to 0.03125
- lib_index: int32 [4, 512, 256], P(None, 'wide', 'narrow'), may hold values from 0 to 7
- tile_map: int32 [4, 512, 256], P(None, 'wide', 'narrow'), may hold values from 0 to 305
- win_x: int32 [16, 8, 4], P('wide', 'narrow'), may hold values from 0 to 31
- win_y: int32 [16, 8, 4], P('wide', 'narrow'), may hold values from 0 to 31
- win_z: int32 [16, 8, 4], P('wide', 'narrow'), may hold values from 0 to 64
Outputs:
- volume: float32 [2, 512, 256, 128], P(None, 'wide', 'narrow')
- correlation: float32 [16, 8, 4, 4096], P('wide', 'narrow')
All inputs are finite; a program needn't handle non-finite values.
Results may differ from a plain program's by a relative error of at most 0.00062.
Values may be sent and summed in bfloat16 or wider, within the bound.
A program may use at most 128 MiB of HBM per device.

v0:
```python
import math

import jax
import jax.numpy as jnp
from jax import lax
from jax.sharding import PartitionSpec as P

WIN = 64
DISP = 16
SWEEPS = 2


def from_behind(value, axis, by):
    devices = lax.axis_size(axis)
    pairs = [(i, i + by) for i in range(devices) if 0 <= i + by < devices]
    return lax.ppermute(value, axis, pairs)


def padded_2(block, sides, width):
    for axis, dim in sides:
        count = lax.axis_size(axis)
        forward = [(i, i + 1) for i in range(count - 1)]
        backward = [(target, source) for source, target in forward]
        low = lax.ppermute(
            lax.slice_in_dim(block, block.shape[dim] - width, None, axis=dim), axis, forward
        )
        high = lax.ppermute(lax.slice_in_dim(block, 0, width, axis=dim), axis, backward)
        block = jnp.concatenate([low, block, high], axis=dim)
    return block


def dft_tables():
    indices = jnp.arange(WIN, dtype=jnp.int32)
    full_angle = (
        2.0 * math.pi / WIN * (indices[:, None] * indices[None, :] % WIN).astype(jnp.float32)
    )
    shifts = (jnp.arange(DISP, dtype=jnp.int32) - DISP // 2) % WIN
    part_angle = (
        2.0 * math.pi / WIN * (indices[:, None] * shifts[None, :] % WIN).astype(jnp.float32)
    )
    return (jnp.cos(full_angle), jnp.sin(full_angle), jnp.cos(part_angle), jnp.sin(part_angle))


def turn_axis(real_part, imag_part, cosine, sine_table, form, sign):
    highest = lax.Precision.HIGHEST
    real_cos = jnp.einsum(form, real_part, cosine, precision=highest)
    real_sin = jnp.einsum(form, real_part, sine_table, precision=highest)
    imag_cos = jnp.einsum(form, imag_part, cosine, precision=highest)
    imag_sin = jnp.einsum(form, imag_part, sine_table, precision=highest)
    return (real_cos - sign * imag_sin, imag_cos + sign * real_sin)


def window_correlation(extended, start, tables):
    cosine, sine_table, cos_part, sin_part = tables
    highest = lax.Precision.HIGHEST
    window = lax.dynamic_slice(
        extended, (jnp.int32(0), start[0], start[1], start[2]), (2, WIN, WIN, WIN)
    )
    centred = window - jnp.mean(window, axis=(1, 2, 3), keepdims=True)
    rms = jnp.sqrt(jnp.mean(centred * centred, axis=(1, 2, 3)) + 1e-06)
    stacked = jnp.concatenate([cosine, -sine_table], axis=1)
    first = jnp.einsum("exyz,zk->exyk", centred, stacked, precision=highest)
    real_part = first[..., :WIN]
    imag_part = first[..., WIN:]
    real_part, imag_part = turn_axis(
        real_part, imag_part, cosine, sine_table, "exyk,yq->exqk", -1.0
    )
    real_part, imag_part = turn_axis(
        real_part, imag_part, cosine, sine_table, "exqk,xr->erqk", -1.0
    )
    cross_real = real_part[0] * real_part[1] + imag_part[0] * imag_part[1]
    cross_imag = real_part[0] * imag_part[1] - imag_part[0] * real_part[1]
    cross_real, cross_imag = turn_axis(
        cross_real, cross_imag, cos_part, sin_part, "abk,kd->abd", 1.0
    )
    cross_real, cross_imag = turn_axis(
        cross_real, cross_imag, cos_part, sin_part, "abd,bq->aqd", 1.0
    )
    final = jnp.einsum("aqd,ar->rqd", cross_real, cos_part, precision=highest)
    final = final - jnp.einsum("aqd,ar->rqd", cross_imag, sin_part, precision=highest)
    scale = 1.0 / (WIN**3 * WIN**1.5)
    return (final * scale / (rms[0] * rms[1])).reshape(-1)


def pass_down(carry, unused):
    moved = from_behind(carry, "wide", 1)
    return (moved, moved)


def pass_up(carry, unused):
    moved = from_behind(carry, "wide", -1)
    return (moved, moved)


def body(initial, images, blocks, lib_index, tile_map, win_x, win_y, win_z):
    wide_count = lax.axis_size("wide")
    reach_strips = wide_count // 2
    slot_count = 2 * reach_strips + 1
    own_index = lax.axis_index("wide")
    brick_x, brick_y, voxel_depth = (initial.shape[1], initial.shape[2], initial.shape[3])
    camera_count, tile_rows, tile_cols, pixels = (
        images.shape[1],
        images.shape[2],
        images.shape[3],
        images.shape[4],
    )
    tile_count = tile_rows * tile_cols
    columns = brick_x * brick_y
    library_size = blocks.shape[1]
    highest = lax.Precision.HIGHEST
    volume = initial
    pictures = jnp.log(images.reshape(2, camera_count, tile_count, pixels) + 1.0)
    target_ids = tile_map.reshape(camera_count, columns)
    member_ids = lib_index.reshape(camera_count, columns)
    slot_range = jnp.arange(slot_count * tile_count, dtype=jnp.int32)
    for sweep_index in range(SWEEPS):
        for camera in range(camera_count):
            placement = (target_ids[camera][:, None] == slot_range[None, :]).astype(jnp.float32)
            placement = placement.reshape(columns, slot_count, tile_count)
            chosen = member_ids[camera]
            volume_bf = volume.astype(jnp.bfloat16).reshape(2, columns, voxel_depth)
            column_proj = jnp.zeros((2, columns, pixels), jnp.float32)
            for member in range(library_size):
                product = jnp.einsum(
                    "ebk,pk->ebp",
                    volume_bf,
                    blocks[camera, member],
                    preferred_element_type=jnp.float32,
                )
                column_proj = column_proj + jnp.where(
                    (chosen == member)[None, :, None], product, 0.0
                )
            partial_value = jnp.einsum("bmt,ebp->metp", placement, column_proj, precision=highest)
            padded = jnp.pad(partial_value, ((wide_count, wide_count), (0, 0), (0, 0), (0, 0)))
            outgoing = lax.dynamic_slice_in_dim(
                padded, wide_count - own_index + reach_strips, wide_count, 0
            )
            arrived = lax.all_to_all(outgoing, "wide", split_axis=0, concat_axis=0, tiled=True)
            projection = jnp.sum(arrived, axis=0)
            log_ratio = (pictures[:, camera] - jnp.log(projection + 1.0)).astype(jnp.bfloat16)
            unused_low, below = lax.scan(pass_down, log_ratio, None, length=reach_strips)
            unused_high, above = lax.scan(pass_up, log_ratio, None, length=reach_strips)
            nearby = jnp.concatenate([below[::-1], log_ratio[None], above], axis=0)
            spread = jnp.einsum(
                "bmt,metp->ebp",
                placement.astype(jnp.bfloat16),
                nearby,
                preferred_element_type=jnp.float32,
            )
            spread = spread.astype(jnp.bfloat16)
            back_sum = jnp.zeros((2, columns, voxel_depth), jnp.float32)
            for member in range(library_size):
                product = jnp.einsum(
                    "ebp,pk->ebk",
                    spread,
                    blocks[camera, member],
                    preferred_element_type=jnp.float32,
                )
                back_sum = back_sum + jnp.where((chosen == member)[None, :, None], product, 0.0)
            volume = volume * jnp.exp(back_sum.reshape(2, brick_x, brick_y, voxel_depth))
    extended = padded_2(volume, (("wide", 1), ("narrow", 2)), WIN // 2)
    tables = dft_tables()
    starts = jnp.stack([win_x.reshape(-1), win_y.reshape(-1), win_z.reshape(-1)], axis=1)

    def per_window(start):
        return window_correlation(extended, start, tables)

    results = lax.map(per_window, starts)
    correlation = results.reshape(1, 1, starts.shape[0], DISP * DISP * DISP)
    return (volume, correlation)


def solution(mesh):
    placed = (
        P(None, "wide", "narrow", None),
        P(None, None, "wide", "narrow", None),
        P(),
        P(None, "wide", "narrow"),
        P(None, "wide", "narrow"),
        P("wide", "narrow", None),
        P("wide", "narrow", None),
        P("wide", "narrow", None),
    )
    return jax.shard_map(
        body,
        mesh=mesh,
        in_specs=placed,
        out_specs=(P(None, "wide", "narrow", None), P("wide", "narrow", None, None)),
        check_vma=False,
    )
```

profile of v0, /device:TPU:9, one launch (start us, length us, event | category | flops | bytes accessed | tf_op | source)
XLA Modules:
  0.0 1687.1 jit_solution(14367891287598912199)
XLA Ops:
  24.4 52.4 %while.207 = (s32[]{:T(128)}, bf16[2,18,128]{2,1,0:T(8,128)(2,1)S(1)}, bf16[8,2,18,128]{3,2,0,1:T(8,128)(2,1)S(1)}, s32[]{:T(128)}) while((s32[]{:T(128)}, bf16[2,18,128]{2,1,0:T(8,128)(2,1)S(1)}, bf16[8,2,18,128]{3,2,0,1:T(8,128)(2,1)S(1)}, s32[]{:T(128)}) %tuple.299), condition=%wide.region_2.3_spmd, body=%wide.region_1.2_spmd.sunk | while | flops 2 | bytes 79977 | solution.py:141
  76.8 48.6 %while.208 = (s32[]{:T(128)}, bf16[2,18,128]{2,1,0:T(8,128)(2,1)S(1)}, bf16[8,2,18,128]{3,2,0,1:T(8,128)(2,1)S(1)}, s32[]{:T(128)}) while((s32[]{:T(128)}, bf16[2,18,128]{2,1,0:T(8,128)(2,1)S(1)}, bf16[8,2,18,128]{3,2,0,1:T(8,128)(2,1)S(1)}, s32[]{:T(128)}) %tuple.296), condition=%wide.region_4.5_spmd, body=%wide.region_3.4_spmd.sunk | while | flops 2 | bytes 79977 | solution.py:142
  149.1 53.2 %while.209 = (s32[]{:T(128)}, bf16[2,18,128]{2,1,0:T(8,128)(2,1)S(1)}, bf16[8,2,18,128]{3,2,0,1:T(8,128)(2,1)S(1)}, s32[]{:T(128)}) while((s32[]{:T(128)}, bf16[2,18,128]{2,1,0:T(8,128)(2,1)S(1)}, bf16[8,2,18,128]{3,2,0,1:T(8,128)(2,1)S(1)}, s32[]{:T(128)}) %tuple.305), condition=%wide.region_7.8_spmd, body=%wide.region_6.7_spmd.sunk | while | flops 2 | bytes 79977 | solution.py:141
  202.3 48.6 %while.210 = (s32[]{:T(128)}, bf16[2,18,128]{2,1,0:T(8,128)(2,1)S(1)}, bf16[8,2,18,128]{3,2,0,1:T(8,128)(2,1)S(1)}, s32[]{:T(128)}) while((s32[]{:T(128)}, bf16[2,18,128]{2,1,0:T(8,128)(2,1)S(1)}, bf16[8,2,18,128]{3,2,0,1:T(8,128)(2,1)S(1)}, s32[]{:T(128)}) %tuple.302), condition=%wide.region_9.10_spmd, body=%wide.region_8.9_spmd.sunk | while | flops 2 | bytes 79977 | solution.py:142
  273.1 52.8 %while.211 = (s32[]{:T(128)}, bf16[2,18,128]{2,1,0:T(8,128)(2,1)S(1)}, bf16[8,2,18,128]{3,2,0,1:T(8,128)(2,1)S(1)}, s32[]{:T(128)}) while((s32[]{:T(128)}, bf16[2,18,128]{2,1,0:T(8,128)(2,1)S(1)}, bf16[8,2,18,128]{3,2,0,1:T(8,128)(2,1)S(1)}, s32[]{:T(128)}) %tuple.311), condition=%wide.region_12.13_spmd, body=%wide.region_11.12_spmd.sunk | while | flops 2 | bytes 79977 | solution.py:141
  326.0 48.6 %while.212 = (s32[]{:T(128)}, bf16[2,18,128]{2,1,0:T(8,128)(2,1)S(1)}, bf16[8,2,18,128]{3,2,0,1:T(8,128)(2,1)S(1)}, s32[]{:T(128)}) while((s32[]{:T(128)}, bf16[2,18,128]{2,1,0:T(8,128)(2,1)S(1)}, bf16[8,2,18,128]{3,2,0,1:T(8,128)(2,1)S(1)}, s32[]{:T(128)}) %tuple.308), condition=%wide.region_14.15_spmd, body=%wide.region_13.14_spmd.sunk | while | flops 2 | bytes 79977 | solution.py:142
  398.0 52.4 %while.213 = (s32[]{:T(128)}, bf16[2,18,128]{2,1,0:T(8,128)(2,1)S(1)}, bf16[8,2,18,128]{3,2,0,1:T(8,128)(2,1)S(1)}, s32[]{:T(128)}) while((s32[]{:T(128)}, bf16[2,18,128]{2,1,0:T(8,128)(2,1)S(1)}, bf16[8,2,18,128]{3,2,0,1:T(8,128)(2,1)S(1)}, s32[]{:T(128)}) %tuple.317), condition=%wide.region_17.18_spmd, body=%wide.region_16.17_spmd.sunk | while | flops 2 | bytes 79977 | solution.py:141
  450.5 48.7 %while.214 = (s32[]{:T(128)}, bf16[2,18,128]{2,1,0:T(8,128)(2,1)S(1)}, bf16[8,2,18,128]{3,2,0,1:T(8,128)(2,1)S(1)}, s32[]{:T(128)}) while((s32[]{:T(128)}, bf16[2,18,128]{2,1,0:T(8,128)(2,1)S(1)}, bf16[8,2,18,128]{3,2,0,1:T(8,128)(2,1)S(1)}, s32[]{:T(128)}) %tuple.314), condition=%wide.region_19.20_spmd, body=%wide.region_18.19_spmd.sunk | while | flops 2 | bytes 79977 | solution.py:142
  521.6 52.4 %while.215 = (s32[]{:T(128)}, bf16[2,18,128]{2,1,0:T(8,128)(2,1)S(1)}, bf16[8,2,18,128]{3,2,0,1:T(8,128)(2,1)S(1)}, s32[]{:T(128)}) while((s32[]{:T(128)}, bf16[2,18,128]{2,1,0:T(8,128)(2,1)S(1)}, bf16[8,2,18,128]{3,2,0,1:T(8,128)(2,1)S(1)}, s32[]{:T(128)}) %tuple.323), condition=%wide.region_22.23_spmd, body=%wide.region_21.22_spmd.sunk | while | flops 2 | bytes 79977 | solution.py:141
  574.1 49.4 %while.216 = (s32[]{:T(128)}, bf16[2,18,128]{2,1,0:T(8,128)(2,1)S(1)}, bf16[8,2,18,128]{3,2,0,1:T(8,128)(2,1)S(1)}, s32[]{:T(128)}) while((s32[]{:T(128)}, bf16[2,18,128]{2,1,0:T(8,128)(2,1)S(1)}, bf16[8,2,18,128]{3,2,0,1:T(8,128)(2,1)S(1)}, s32[]{:T(128)}) %tuple.320), condition=%wide.region_24.25_spmd, body=%wide.region_23.24_spmd.sunk | while | flops 2 | bytes 79977 | solution.py:142
  646.1 52.4 %while.217 = (s32[]{:T(128)}, bf16[2,18,128]{2,1,0:T(8,128)(2,1)S(1)}, bf16[8,2,18,128]{3,2,0,1:T(8,128)(2,1)S(1)}, s32[]{:T(128)}) while((s32[]{:T(128)}, bf16[2,18,128]{2,1,0:T(8,128)(2,1)S(1)}, bf16[8,2,18,128]{3,2,0,1:T(8,128)(2,1)S(1)}, s32[]{:T(128)}) %tuple.329), condition=%wide.region_27.28_spmd, body=%wide.region_26.27_spmd.sunk | while | flops 2 | bytes 79977 | solution.py:141
  698.6 48.9 %while.218 = (s32[]{:T(128)}, bf16[2,18,128]{2,1,0:T(8,128)(2,1)S(1)}, bf16[8,2,18,128]{3,2,0,1:T(8,128)(2,1)S(1)}, s32[]{:T(128)}) while((s32[]{:T(128)}, bf16[2,18,128]{2,1,0:T(8,128)(2,1)S(1)}, bf16[8,2,18,128]{3,2,0,1:T(8,128)(2,1)S(1)}, s32[]{:T(128)}) %tuple.326), condition=%wide.region_29.30_spmd, body=%wide.region_28.29_spmd.sunk | while | flops 2 | bytes 79977 | solution.py:142
  771.2 52.4 %while.219 = (s32[]{:T(128)}, bf16[2,18,128]{2,1,0:T(8,128)(2,1)S(1)}, bf16[8,2,18,128]{3,2,0,1:T(8,128)(2,1)S(1)}, s32[]{:T(128)}) while((s32[]{:T(128)}, bf16[2,18,128]{2,1,0:T(8,128)(2,1)S(1)}, bf16[8,2,18,128]{3,2,0,1:T(8,128)(2,1)S(1)}, s32[]{:T(128)}) %tuple.335), condition=%wide.region_32.33_spmd, body=%wide.region_31.32_spmd.sunk | while | flops 2 | bytes 79977 | solution.py:141
  823.7 48.6 %while.220 = (s32[]{:T(128)}, bf16[2,18,128]{2,1,0:T(8,128)(2,1)S(1)}, bf16[8,2,18,128]{3,2,0,1:T(8,128)(2,1)S(1)}, s32[]{:T(128)}) while((s32[]{:T(128)}, bf16[2,18,128]{2,1,0:T(8,128)(2,1)S(1)}, bf16[8,2,18,128]{3,2,0,1:T(8,128)(2,1)S(1)}, s32[]{:T(128)}) %tuple.332), condition=%wide.region_34.35_spmd, body=%wide.region_33.34_spmd.sunk | while | flops 2 | bytes 79977 | solution.py:142
  894.3 52.5 %while.221 = (s32[]{:T(128)}, bf16[2,18,128]{2,1,0:T(8,128)(2,1)S(1)}, bf16[8,2,18,128]{3,2,0,1:T(8,128)(2,1)S(1)}, s32[]{:T(128)}) while((s32[]{:T(128)}, bf16[2,18,128]{2,1,0:T(8,128)(2,1)S(1)}, bf16[8,2,18,128]{3,2,0,1:T(8,128)(2,1)S(1)}, s32[]{:T(128)}) %tuple.341), condition=%wide.region_37.38_spmd, body=%wide.region_36.37_spmd.sunk | while | flops 2 | bytes 79977 | solution.py:141
  946.9 48.7 %while.222 = (s32[]{:T(128)}, bf16[2,18,128]{2,1,0:T(8,128)(2,1)S(1)}, bf16[8,2,18,128]{3,2,0,1:T(8,128)(2,1)S(1)}, s32[]{:T(128)}) while((s32[]{:T(128)}, bf16[2,18,128]{2,1,0:T(8,128)(2,1)S(1)}, bf16[8,2,18,128]{3,2,0,1:T(8,128)(2,1)S(1)}, s32[]{:T(128)}) %tuple.338), condition=%wide.region_39.40_spmd, body=%wide.region_38.39_spmd.sunk | while | flops 2 | bytes 79977 | solution.py:142
  1007.2 9.9 collective-permute-done.17
  1024.9 158.7 %collective-permute-start.19 = (f32[2,96,32,128]{3,2,1,0:T(8,128)}, f32[2,96,32,128]{3,2,1,0:T(8,128)}, u32[]{:S(2)}, u32[]{:S(2)}) collective-permute-start(f32[2,96,32,128]{3,2,1,0:T(8,128)} %pad_maximum_fusion.1), channel_id=1, source_target_pairs={{1,0},{2,1},{3,2},{4,3},{5,4},{6,5},{7,6},{9,8},{10,9},{11,10},{12... | collective-permute-start | bytes 9437192 | tf_op jit(solution)/shard_map/ppermute | solution.py:27
  1187.4 32.9 %collective-permute-done.19 = f32[2,96,32,128]{3,2,1,0:T(8,128)} collective-permute-done((f32[2,96,32,128]{3,2,1,0:T(8,128)}, f32[2,96,32,128]{3,2,1,0:T(8,128)}, u32[]{:S(2)}, u32[]{:S(2)}) %collective-permute-start.19) | collective-permute-done | bytes 3145760 | tf_op jit(solution)/shard_map/ppermute | solution.py:27
  1227.4 458.5 %while.223 = (s32[]{:T(128)}, f32[4,4096]{1,0:T(4,128)S(1)}, s32[4,3]{1,0:T(4,128)S(1)}, f32[2,96,96,128]{3,2,1,0:T(8,128)}, f32[64,128]{1,0:T(8,128)S(1)}, /*in...) while((s32[]{:T(128)}, f32[4,4096]{1,0:T(4,128)S(1)}, ...), condition=%wide.region_43.44_spmd.clone.clone.clone, body=%wide.region_40.43_spmd.clone.clone.clone.sunk | while | flops 4293648384 | bytes 136496256 | solution.py:168
  1249.2 8.1 fusion.995
  1257.3 9.1 subtract_bitcast_fusion.4
  1287.0 8.7 add_bitcast_fusion.4
  1353.1 8.1 fusion.995
  1361.2 23.0 %subtract_bitcast_fusion.4 = f32[2,64,64,64]{2,3,1,0:T(8,128)} fusion(f32[2,64,64,64]{3,2,1,0:T(8,128)S(1)} %fusion.995, f32[2,64,64,128]{3,2,1,0:T(8,128)S(1)} %fusion.992), kind=kOutput, calls=%fused_computation.24.clone.1 | convolution fusion | flops 403759104 | bytes 8388608 | tf_op jit(solution)/shard_map/while/body/eval_jaxpr/exyk,yq->exqk/dot_general | solution.py:46
  1404.8 8.7 add_bitcast_fusion.4
  1471.0 8.1 fusion.995
  1479.1 23.0 %subtract_bitcast_fusion.4 = f32[2,64,64,64]{2,3,1,0:T(8,128)} fusion(f32[2,64,64,64]{3,2,1,0:T(8,128)S(1)} %fusion.995, f32[2,64,64,128]{3,2,1,0:T(8,128)S(1)} %fusion.992), kind=kOutput, calls=%fused_computation.24.clone.1 | convolution fusion | flops 403759104 | bytes 8388608 | tf_op jit(solution)/shard_map/while/body/eval_jaxpr/exyk,yq->exqk/dot_general | solution.py:46
  1522.8 8.7 add_bitcast_fusion.4
  1588.9 8.1 fusion.995
  1597.1 23.0 %subtract_bitcast_fusion.4 = f32[2,64,64,64]{2,3,1,0:T(8,128)} fusion(f32[2,64,64,64]{3,2,1,0:T(8,128)S(1)} %fusion.995, f32[2,64,64,128]{3,2,1,0:T(8,128)S(1)} %fusion.992), kind=kOutput, calls=%fused_computation.24.clone.1 | convolution fusion | flops 403759104 | bytes 8388608 | tf_op jit(solution)/shard_map/while/body/eval_jaxpr/exyk,yq->exqk/dot_general | solution.py:46
  1640.7 8.7 add_bitcast_fusion.4
  (988 shorter events, 1305.3 us)
Async XLA Ops:
  11.3 12.9 all-to-all-start
  24.4 6.5 collective-permute-start
  30.9 6.5 collective-permute-start
  44.0 6.5 collective-permute-start
  50.6 6.5 collective-permute-start
  63.7 6.5 collective-permute-start
  99.2 6.6 collective-permute-start.1
  134.9 14.0 all-to-all-start.1
  149.1 6.5 collective-permute-start.2
  162.2 7.3 collective-permute-start.2
  259.4 13.5 all-to-all-start.2
  273.1 6.5 collective-permute-start.4
  305.9 7.0 collective-permute-start.4
  384.0 13.8 all-to-all-start.3
  398.0 6.5 collective-permute-start.6
  507.7 13.8 all-to-all-start.4
  521.6 6.5 collective-permute-start.8
  596.5 7.3 collective-permute-start.9
  632.9 13.0 all-to-all-start.5
  646.2 6.5 collective-permute-start.10
  740.7 6.9 collective-permute-start.11
  757.0 14.0 all-to-all-start.6
  771.2 6.5 collective-permute-start.12
  833.0 6.6 collective-permute-start.13
  880.8 13.3 all-to-all-start.7
  894.3 6.5 collective-permute-start.14
  920.5 6.7 collective-permute-start.14
  969.3 6.6 collective-permute-start.15
  999.5 17.6 %collective-permute-start.17 = (f32[2,32,32,128]{3,2,1,0:T(8,128)S(1)}, f32[2,32,32,128]{3,2,1,0:T(8,128)S(1)}, u32[]{:S(2)}, u32[]{:S(2)}) collective-permute-start(f32[2,32,32,128]{3,2,1,0:T(8,128)S(1)} %mul.280), channel_id=1, source_target_pairs={{8,0},{16,8},{24,16},{32,24},{40,32},{48,40},{56,48},{64,56},{72,6... | collective-permute-start | bytes 3145736 | tf_op jit(solution)/shard_map/ppermute | solution.py:27
  1005.3 17.7 %collective-permute-start.16 = (f32[2,32,32,128]{3,2,1,0:T(8,128)S(1)}, f32[2,32,32,128]{3,2,1,0:T(8,128)S(1)}, u32[]{:S(2)}, u32[]{:S(2)}) collective-permute-start(f32[2,32,32,128]{3,2,1,0:T(8,128)S(1)} %mul.280), channel_id=1, source_target_pairs={{0,8},{8,16},{16,24},{24,32},{32,40},{40,48},{48,56},{56,64},{64,7... | collective-permute-start | bytes 3145736 | tf_op jit(solution)/shard_map/ppermute | solution.py:24
  1024.9 195.5 %collective-permute-start.19 = (f32[2,96,32,128]{3,2,1,0:T(8,128)}, f32[2,96,32,128]{3,2,1,0:T(8,128)}, u32[]{:S(2)}, u32[]{:S(2)}) collective-permute-start(f32[2,96,32,128]{3,2,1,0:T(8,128)} %pad_maximum_fusion.1), channel_id=1, source_target_pairs={{1,0},{2,1},{3,2},{4,3},{5,4},{6,5},{7,6},{9,8},{10,9},{11,10},{12... | collective-permute-start | bytes 9437192 | tf_op jit(solution)/shard_map/ppermute | solution.py:27
  1183.5 38.0 %collective-permute-start.18 = (f32[2,96,32,128]{3,2,1,0:T(8,128)}, f32[2,96,32,128]{3,2,1,0:T(8,128)}, u32[]{:S(2)}, u32[]{:S(2)}) collective-permute-start(f32[2,96,32,128]{3,2,1,0:T(8,128)} %pad_maximum_fusion.1), channel_id=1, source_target_pairs={{0,1},{1,2},{2,3},{3,4},{4,5},{5,6},{6,7},{8,9},{9,10},{10,11},{11... | collective-permute-start | bytes 9437192 | tf_op jit(solution)/shard_map/ppermute | solution.py:24
  (136 other events, 1597.5 us)
where the time goes:
time: 1700 us; the launch traced here: 1690 us
  starting transfers between devices  676 us (40%)
  waiting for transfers between devices  458 us (27%)
  matrix products  398 us (23%)
  local copies, waits for them, and re-layouts  68.3 us (4%)
  other arithmetic  52.5 us (3%)
  loops' own time  32.2 us (2%)
    ppermute x128, starting transfers between devices, from_behind(): return lax.ppermute(value, axis, pairs)  445 us
    ppermute x128, waiting for transfers between devices, from_behind(): return lax.ppermute(value, axis, pairs)  363 us
    ppermute x2, starting transfers between devices, padded_2(): lax.ppermute(lax.slice_in_dim(block, 0, width, axis=dim), axis, backward)  164 us
    dot_general x16, matrix products, turn_axis(): real_cos = jnp.einsum(form, real_part, cosine, precision=highest)  118 us
    dot_general x16, matrix products, turn_axis(): imag_sin = jnp.einsum(form, imag_part, sine_table, precision=highest)  75.6 us
    dot_general x16, matrix products, turn_axis(): real_sin = jnp.einsum(form, real_part, sine_table, precision=highest)  60.5 us
    all_to_all x8, starting transfers between devices, body(): lax.all_to_all(outgoing, 'wide', split_axis=0, concat_axis=0, tiled=True)  60.3 us
    dot_general x16, matrix products, turn_axis(): imag_cos = jnp.einsum(form, imag_part, cosine, precision=highest)  57.7 us
  transfers between devices with their start and end apart: 140, of which 140 were waited for; matrix products, arithmetic and copies ran while one was open for 0% of the time, Pallas kernels for 0%

commit v1 on v0

v1 whole, which is shorter than its diff:
```python
import functools
import math

import jax
import jax.numpy as jnp
from jax import lax
from jax.experimental import pallas as pl
from jax.experimental.pallas import tpu as pltpu
from jax.sharding import PartitionSpec as P

MESH = pl.DeviceIdType.MESH
PROJ_ROWS = 24
RATIO_ROWS = 32
CHUNK = 256
WIN = 64
DISP = 16
SWEEPS = 2


def padded_2(block, sides, width):
    for axis, dim in sides:
        count = lax.axis_size(axis)
        forward = [(i, i + 1) for i in range(count - 1)]
        backward = [(target, source) for source, target in forward]
        low = lax.ppermute(
            lax.slice_in_dim(block, block.shape[dim] - width, None, axis=dim), axis, forward
        )
        high = lax.ppermute(lax.slice_in_dim(block, 0, width, axis=dim), axis, backward)
        block = jnp.concatenate([low, block, high], axis=dim)
    return block


def dft_tables():
    indices = jnp.arange(WIN, dtype=jnp.int32)
    full_angle = (
        2.0 * math.pi / WIN * (indices[:, None] * indices[None, :] % WIN).astype(jnp.float32)
    )
    shifts = (jnp.arange(DISP, dtype=jnp.int32) - DISP // 2) % WIN
    part_angle = (
        2.0 * math.pi / WIN * (indices[:, None] * shifts[None, :] % WIN).astype(jnp.float32)
    )
    return (jnp.cos(full_angle), jnp.sin(full_angle), jnp.cos(part_angle), jnp.sin(part_angle))


def turn_axis(real_part, imag_part, cosine, sine_table, form, sign):
    highest = lax.Precision.HIGHEST
    real_cos = jnp.einsum(form, real_part, cosine, precision=highest)
    real_sin = jnp.einsum(form, real_part, sine_table, precision=highest)
    imag_cos = jnp.einsum(form, imag_part, cosine, precision=highest)
    imag_sin = jnp.einsum(form, imag_part, sine_table, precision=highest)
    return (real_cos - sign * imag_sin, imag_cos + sign * real_sin)


def window_correlation(extended, start, tables):
    cosine, sine_table, cos_part, sin_part = tables
    highest = lax.Precision.HIGHEST
    window = lax.dynamic_slice(
        extended, (jnp.int32(0), start[0], start[1], start[2]), (2, WIN, WIN, WIN)
    )
    centred = window - jnp.mean(window, axis=(1, 2, 3), keepdims=True)
    rms = jnp.sqrt(jnp.mean(centred * centred, axis=(1, 2, 3)) + 1e-06)
    stacked = jnp.concatenate([cosine, -sine_table], axis=1)
    first = jnp.einsum("exyz,zk->exyk", centred, stacked, precision=highest)
    real_part = first[..., :WIN]
    imag_part = first[..., WIN:]
    real_part, imag_part = turn_axis(
        real_part, imag_part, cosine, sine_table, "exyk,yq->exqk", -1.0
    )
    real_part, imag_part = turn_axis(
        real_part, imag_part, cosine, sine_table, "exqk,xr->erqk", -1.0
    )
    cross_real = real_part[0] * real_part[1] + imag_part[0] * imag_part[1]
    cross_imag = real_part[0] * imag_part[1] - imag_part[0] * real_part[1]
    cross_real, cross_imag = turn_axis(
        cross_real, cross_imag, cos_part, sin_part, "abk,kd->abd", 1.0
    )
    cross_real, cross_imag = turn_axis(
        cross_real, cross_imag, cos_part, sin_part, "abd,bq->aqd", 1.0
    )
    final = jnp.einsum("aqd,ar->rqd", cross_real, cos_part, precision=highest)
    final = final - jnp.einsum("aqd,ar->rqd", cross_imag, sin_part, precision=highest)
    scale = 1.0 / (WIN**3 * WIN**1.5)
    return (final * scale / (rms[0] * rms[1])).reshape(-1)


def sweeps_kernel(
    init_ref, img_ref, fwd_ref, bwd_ref, lib_ref, gather_ref, spread_ref,
    vol_ref,
    cols_ref, part_ref, recv_ref, ratio_ref,
    part_send, part_recv, ratio_send, ratio_recv,
):
    count = lax.axis_size("wide")
    me = lax.axis_index("wide")
    cams, members = fwd_ref.shape[0], fwd_ref.shape[1] // 128
    columns = init_ref.shape[1]

    barrier = pltpu.get_barrier_semaphore()

    def greet(d, _):
        pl.semaphore_signal(
            barrier, inc=1, device_id={"wide": lax.rem(me + d, count)}, device_id_type=MESH
        )
        return 0

    lax.fori_loop(1, count, greet, 0)

    def masked(values, lib):
        return jnp.concatenate(
            [jnp.where(lib == m, values, jnp.zeros_like(values)) for m in range(members)], axis=1
        )

    def project_rows(e, cam, rows, vol):
        lhs = masked(vol.astype(jnp.bfloat16), lib_ref[cam, rows, :])
        proj = jnp.dot(lhs, fwd_ref[cam], preferred_element_type=jnp.float32)
        high = proj.astype(jnp.bfloat16)
        low = (proj - high.astype(jnp.float32)).astype(jnp.bfloat16)
        cols_ref[e, rows, 0:128] = high
        cols_ref[e, rows, 128:256] = low

    def part_copy(e, d):
        target = lax.rem(me + d, count)
        return pltpu.make_async_remote_copy(
            src_ref=part_ref.at[e, target],
            dst_ref=recv_ref.at[e, me],
            send_sem=part_send.at[e, d],
            recv_sem=part_recv.at[e, me],
            device_id={"wide": target},
            device_id_type=MESH,
        )

    def part_arrival(e, d):
        source = lax.rem(me + d, count)
        return pltpu.make_async_remote_copy(
            src_ref=part_ref.at[e, source],
            dst_ref=recv_ref.at[e, source],
            send_sem=part_send.at[e, d],
            recv_sem=part_recv.at[e, source],
            device_id={"wide": source},
            device_id_type=MESH,
        )

    def strip(e, owner):
        return ratio_ref.at[e, pl.ds(pl.multiple_of(owner * RATIO_ROWS, RATIO_ROWS), RATIO_ROWS)]

    def ratio_copy(e, d):
        target = lax.rem(me + d, count)
        return pltpu.make_async_remote_copy(
            src_ref=strip(e, me),
            dst_ref=strip(e, me),
            send_sem=ratio_send.at[e, d],
            recv_sem=ratio_recv.at[e, me],
            device_id={"wide": target},
            device_id_type=MESH,
        )

    def ratio_arrival(e, d):
        source = lax.rem(me + d, count)
        return pltpu.make_async_remote_copy(
            src_ref=strip(e, me),
            dst_ref=strip(e, source),
            send_sem=ratio_send.at[e, d],
            recv_sem=ratio_recv.at[e, source],
            device_id={"wide": source},
            device_id_type=MESH,
        )

    def each(action):
        def step(d, _):
            action(d)
            return 0

        lax.fori_loop(1, count, step, 0)

    def send_parts(e, cam):
        both = jnp.dot(gather_ref[cam], cols_ref[e], preferred_element_type=jnp.float32)
        total = both[:, 0:128] + both[:, 128:256]
        part_ref[e] = total.reshape(part_ref.shape[1:])
        each(lambda d: part_copy(e, d).start())

    def send_ratio(e, cam):
        def take(d, total):
            part_arrival(e, d).wait_recv()
            return total + recv_ref[e, lax.rem(me + d, count)]

        total = lax.fori_loop(1, count, take, part_ref[e, me])
        ratio = jnp.log(img_ref[e, cam] + 1.0) - jnp.log(total + 1.0)
        ratio = jnp.concatenate(
            [ratio, jnp.zeros((RATIO_ROWS - PROJ_ROWS, 128), jnp.float32)], axis=0
        )
        ratio_ref[e, pl.ds(pl.multiple_of(me * RATIO_ROWS, RATIO_ROWS), RATIO_ROWS), :] = (
            ratio.astype(jnp.bfloat16)
        )
        each(lambda d: ratio_copy(e, d).start())

    def collect_ratio(e):
        each(lambda d: ratio_arrival(e, d).wait_recv())
        each(lambda d: part_copy(e, d).wait_send())
        each(lambda d: ratio_copy(e, d).wait_send())

    def updated_rows(e, cam, rows):
        near = jnp.dot(spread_ref[cam, rows, :], ratio_ref[e], preferred_element_type=jnp.float32)
        lhs = masked(near.astype(jnp.bfloat16), lib_ref[cam, rows, :])
        back = jnp.dot(lhs, bwd_ref[cam], preferred_element_type=jnp.float32)
        return vol_ref[e, rows, :] * jnp.exp(back)

    def chunks(action):
        def step(i, _):
            action(pl.ds(pl.multiple_of(i * CHUNK, CHUNK), CHUNK))
            return 0

        lax.fori_loop(0, columns // CHUNK, step, 0, unroll=2)

    for e in range(2):
        def first(rows):
            vol = init_ref[e, rows, :]
            vol_ref[e, rows, :] = vol
            project_rows(e, 0, rows, vol)

        chunks(first)
        if e == 0:
            pl.semaphore_wait(barrier, count - 1)
        send_parts(e, 0)

    def round_step(r, _):
        cam = lax.rem(r, cams)
        following = lax.rem(r + 1, cams)
        for e in range(2):
            send_ratio(e, cam)
        for e in range(2):
            collect_ratio(e)

            def both(rows):
                vol = updated_rows(e, cam, rows)
                vol_ref[e, rows, :] = vol
                project_rows(e, following, rows, vol)

            chunks(both)
            send_parts(e, following)
        return 0

    last = SWEEPS * cams - 1
    lax.fori_loop(0, last, round_step, 0)
    for e in range(2):
        send_ratio(e, cams - 1)
    for e in range(2):
        collect_ratio(e)

        def final(rows):
            vol_ref[e, rows, :] = updated_rows(e, cams - 1, rows)

        chunks(final)


def reconstruct(initial, images, blocks, lib_index, tile_map):
    count = lax.axis_size("wide")
    own = lax.axis_index("wide")
    cams, members = blocks.shape[0], blocks.shape[1]
    columns = initial.shape[1] * initial.shape[2]
    tiles = images.shape[2] * images.shape[3]
    ids = tile_map.reshape(cams, columns)
    strips = own - count // 2 + ids // tiles
    inside = (strips >= 0) & (strips < count)
    gather_ids = jnp.where(inside, strips * PROJ_ROWS + ids % tiles, -1)
    spread_ids = jnp.where(inside, strips * RATIO_ROWS + ids % tiles, -1)
    gather = gather_ids[:, None, :] == lax.broadcasted_iota(
        jnp.int32, (cams, count * PROJ_ROWS, columns), 1
    )
    spread = spread_ids[:, :, None] == lax.broadcasted_iota(
        jnp.int32, (cams, columns, count * RATIO_ROWS), 2
    )
    lib = jnp.broadcast_to(lib_index.reshape(cams, columns, 1), (cams, columns, 128))
    backward = blocks.reshape(cams, members * 128, 128)
    forward = blocks.transpose(0, 1, 3, 2).reshape(cams, members * 128, 128)
    pictures = jnp.pad(
        images.reshape(2, cams, tiles, 128), ((0, 0), (0, 0), (0, PROJ_ROWS - tiles), (0, 0))
    )
    vmem = pl.BlockSpec(memory_space=pltpu.VMEM)
    return pl.pallas_call(
        sweeps_kernel,
        out_shape=jax.ShapeDtypeStruct((2, columns, 128), jnp.float32),
        in_specs=[vmem] * 7,
        out_specs=vmem,
        scratch_shapes=[
            pltpu.VMEM((2, columns, 256), jnp.bfloat16),
            pltpu.VMEM((2, count, PROJ_ROWS, 128), jnp.float32),
            pltpu.VMEM((2, count, PROJ_ROWS, 128), jnp.float32),
            pltpu.VMEM((2, count * RATIO_ROWS, 128), jnp.bfloat16),
            pltpu.SemaphoreType.DMA((2, count)),
            pltpu.SemaphoreType.DMA((2, count)),
            pltpu.SemaphoreType.DMA((2, count)),
            pltpu.SemaphoreType.DMA((2, count)),
        ],
        compiler_params=pltpu.CompilerParams(
            collective_id=0, has_side_effects=True, vmem_limit_bytes=48 * 1024 * 1024
        ),
        name="sweeps",
    )(
        initial.reshape(2, columns, 128),
        pictures,
        forward,
        backward,
        lib.astype(jnp.bfloat16),
        gather.astype(jnp.bfloat16),
        spread.astype(jnp.bfloat16),
    ).reshape(initial.shape)


def body(initial, images, blocks, lib_index, tile_map, win_x, win_y, win_z):
    volume = reconstruct(initial, images, blocks, lib_index, tile_map)
    extended = padded_2(volume, (("wide", 1), ("narrow", 2)), WIN // 2)
    tables = dft_tables()
    starts = jnp.stack([win_x.reshape(-1), win_y.reshape(-1), win_z.reshape(-1)], axis=1)

    def per_window(start):
        return window_correlation(extended, start, tables)

    results = lax.map(per_window, starts)
    correlation = results.reshape(1, 1, starts.shape[0], DISP * DISP * DISP)
    return (volume, correlation)


def solution(mesh):
    placed = (
        P(None, "wide", "narrow", None),
        P(None, None, "wide", "narrow", None),
        P(),
        P(None, "wide", "narrow"),
        P(None, "wide", "narrow"),
        P("wide", "narrow", None),
        P("wide", "narrow", None),
        P("wide", "narrow", None),
    )
    return jax.shard_map(
        body,
        mesh=mesh,
        in_specs=placed,
        out_specs=(P(None, "wide", "narrow", None), P("wide", "narrow", None, None)),
        check_vma=False,
    )
```

time: 1700 us -> 738 us (0.43)
  starting transfers between devices: 676 us -> 26.9 us
  waiting for transfers between devices: 458 us -> 50.3 us
  Pallas kernels: 0 us -> 110 us
  matrix products: 398 us -> 367 us
    ppermute x128 -> x0, starting transfers between devices: 445 us -> none  [from_behind(): return lax.ppermute(value, axis, pairs)]
    ppermute x128 -> x0, waiting for transfers between devices: 363 us -> none  [from_behind(): return lax.ppermute(value, axis, pairs)]
    ppermute x2, starting transfers between devices: 164 us -> 21.6 us  [padded_2(): lax.ppermute(lax.slice_in_dim(block, 0, width, axis=dim), axis, backward)]
    pallas_call x0 -> x1, Pallas kernels: none -> 110 us  [reconstruct(): pl.pallas_call(sweeps_kernel, out_shape=jax.ShapeDtypeStruct((2, columns,...]
    all_to_all x8 -> x0, starting transfers between devices: 60.3 us -> none  [body(): lax.all_to_all(outgoing, 'wide', split_axis=0, concat_axis=0, tiled=True)]
    dot_general x144 -> x0, matrix products: 58.4 us -> none  [the longest x64 24.4 us: body(): jnp.einsum('ebp,pk->ebk', spread, blocks[camera, member], preferred_eleme...]
    all_to_all x8 -> x0, waiting for transfers between devices: 45.6 us -> none  [body(): lax.all_to_all(outgoing, 'wide', split_axis=0, concat_axis=0, tiled=True)]
    dot_general x0 -> x16, local copies, waits for them, and re-layouts: none -> 28.4 us  [the longest x4 8.69 us: turn_axis(): imag_sin = jnp.einsum(form, imag_part, sine_table, precision=highest)]
  transfers between devices with their start and end apart: 140 -> 4, of which waited for: 140 -> 4; matrix products, arithmetic and copies ran while one was open for 0% -> 0% of each run, Pallas kernels for 0% -> 0%
where the time goes in v1:
time: 738 us; the launch traced here: 728 us
  matrix products  367 us (50%)
  Pallas kernels  110 us (15%)
  local copies, waits for them, and re-layouts  84.8 us (11%)
  other arithmetic  58.5 us (8%)
  waiting for transfers between devices  50.3 us (7%)
  loops' own time  29.3 us (4%)
  starting transfers between devices  26.9 us (4%)
    dot_general x16, matrix products, turn_axis(): real_cos = jnp.einsum(form, real_part, cosine, precision=highest)  135 us
    pallas_call x1, Pallas kernels, reconstruct(): pl.pallas_call(sweeps_kernel, out_shape=jax.ShapeDtypeStruct((2, columns,...  110 us
    dot_general x16, matrix products, turn_axis(): imag_sin = jnp.einsum(form, imag_part, sine_table, precision=highest)  79.4 us
    dot_general x16, matrix products, turn_axis(): real_sin = jnp.einsum(form, real_part, sine_table, precision=highest)  63.8 us
    dot_general x16, matrix products, turn_axis(): imag_cos = jnp.einsum(form, imag_part, cosine, precision=highest)  61.1 us
    ppermute x2, waiting for transfers between devices, padded_2(): lax.ppermute(lax.slice_in_dim(block, 0, width, axis=dim), axis, backward)  44.2 us
    another operation x1, loops' own time, body(): results = lax.map(per_window, starts)  29.3 us
    dot_general x4, matrix products, window_correlation(): first = jnp.einsum('exyz,zk->exyk', centred, stacked, precision=highest)  24.8 us
  transfers between devices with their start and end apart: 4, of which 4 were waited for; matrix products, arithmetic and copies ran while one was open for 0% of the time, Pallas kernels for 0%

profile of v1, /device:TPU:9, one launch (start us, length us, event | category | flops | bytes accessed | tf_op | source)
XLA Modules:
  0.0 727.9 jit_solution(8415080450877013869)
XLA Ops:
  12.1 109.6 %sweeps.1 = f32[2,1024,128]{2,1,0:T(8,128)S(1)} custom-call(f32[2,1024,128]{2,1,0:T(8,128)S(1)} %bitcast.177, f32[2,4,24,128]{3,2,1,0:T(8,128)S(1)} %pad.4.img_ref, bf16[4,1024,128]{2,1,0:T(8,128)(2,1)S(1)} %bitcast.176, bf16[4,1024,128]{2,1,0:T(8,128)(2,1)S(1)} %bitcast.175, bf16[4,1024,128]{2,1,0:T(8,128)(2,1)S(1)} %broadcast_in_dim.12.lib_ref, ...), custom_call_target="tpu_custom_call" | custom-call | tf_op jit(solution)/shard_map/sweeps/pallas_call | solution.py:278
  127.6 11.3 %collective-permute-done.1 = f32[2,32,32,128]{3,2,1,0:T(8,128)S(1)} collective-permute-done((f32[2,32,32,128]{3,2,1,0:T(8,128)S(1)}, f32[2,32,32,128]{3,2,1,0:T(8,128)S(1)}, u32[]{:S(2)}, u32[]{:S(2)}) %collective-permute-start.1) | collective-permute-done | bytes 1048608 | tf_op jit(solution)/shard_map/ppermute | solution.py:28
  145.7 17.8 %collective-permute-start.3 = (f32[2,96,32,128]{3,2,1,0:T(8,128)}, f32[2,96,32,128]{3,2,1,0:T(8,128)}, u32[]{:S(2)}, u32[]{:S(2)}) collective-permute-start(f32[2,96,32,128]{3,2,1,0:T(8,128)} %pad_maximum_fusion.1), channel_id=1, source_target_pairs={{1,0},{2,1},{3,2},{4,3},{5,4},{6,5},{7,6},{9,8},{10,9},{11,10},{12... | collective-permute-start | bytes 9437192 | tf_op jit(solution)/shard_map/ppermute | solution.py:28
  167.3 32.9 %collective-permute-done.3 = f32[2,96,32,128]{3,2,1,0:T(8,128)} collective-permute-done((f32[2,96,32,128]{3,2,1,0:T(8,128)}, f32[2,96,32,128]{3,2,1,0:T(8,128)}, u32[]{:S(2)}, u32[]{:S(2)}) %collective-permute-start.3) | collective-permute-done | bytes 3145760 | tf_op jit(solution)/shard_map/ppermute | solution.py:28
  207.3 519.4 %while.15 = (s32[]{:T(128)}, f32[4,4096]{1,0:T(4,128)S(1)}, s32[4,3]{1,0:T(4,128)S(1)}, f32[2,96,96,128]{3,2,1,0:T(8,128)}, f32[64,128]{1,0:T(8,128)S(1)}, /*ind...) while((s32[]{:T(128)}, f32[4,4096]{1,0:T(4,128)S(1)}, ...), condition=%wide.region_3.4_spmd.clone.clone.clone, body=%wide.region_0.3_spmd.clone.clone.clone.sunk | while | flops 4293648384 | bytes 138593424 | solution.py:317
  222.5 6.3 fusion.287
  228.8 8.1 %fusion.290 = f32[2,64,64,64]{3,2,1,0:T(8,128)S(1)} fusion(f32[2,64,64,128]{3,2,1,0:T(8,128)S(1)} %fusion.287), kind=kOutput, calls=%fused_computation.11.clone.1 | convolution fusion | flops 402710528 | bytes 6291456 | tf_op jit(solution)/shard_map/while/body/eval_jaxpr/exyk,yq->exqk/dot_general | solution.py:50
  237.0 23.2 %subtract_bitcast_fusion.4 = f32[2,64,64,64]{2,3,1,0:T(8,128)} fusion(f32[2,64,64,64]{3,2,1,0:T(8,128)S(1)} %fusion.290, f32[2,64,64,128]{3,2,1,0:T(8,128)S(1)} %fusion.287), kind=kOutput, calls=%fused_computation.8.clone.1 | convolution fusion | flops 403759104 | bytes 8388608 | tf_op jit(solution)/shard_map/while/body/eval_jaxpr/exyk,yq->exqk/dot_general | solution.py:47
  265.7 7.0 fusion.291
  272.8 8.0 %fusion.288 = f32[2,64,64,64]{3,2,1,0:T(8,128)S(1)} fusion(f32[2,64,64,128]{3,2,1,0:T(8,128)S(1)} %copy-done.5), kind=kOutput, calls=%fused_computation.9.clone.1 | convolution fusion | flops 402710528 | bytes 6291456 | tf_op jit(solution)/shard_map/while/body/eval_jaxpr/exyk,yq->exqk/dot_general | solution.py:49
  280.8 8.7 %add_bitcast_fusion.4 = f32[2,64,64,64]{2,3,1,0:T(8,128)} fusion(f32[2,64,64,64]{3,2,1,0:T(8,128)S(1)} %fusion.288, f32[2,64,64,128]{3,2,1,0:T(8,128)S(1)} %copy-done.5), kind=kOutput, calls=%fused_computation.7.clone.1 | convolution fusion | flops 403759104 | bytes 8388608 | tf_op jit(solution)/shard_map/while/body/eval_jaxpr/exyk,yq->exqk/dot_general | solution.py:48
  295.1 8.2 %subtract_bitcast_fusion.5 = f32[2,64,64,64]{1,3,2,0:T(8,128)S(1)} fusion(f32[2,64,64,64]{3,2,1,0:T(8,128)} %fusion.291, f32[2,64,64,64]{1,3,2,0:T(8,128)} %copy.109), kind=kOutput, calls=%fused_computation.6.clone.1 | convolution fusion | flops 403759104 | bytes 6291456 | tf_op jit(solution)/shard_map/while/body/eval_jaxpr/exqk,xr->erqk/dot_general | solution.py:50
  352.3 6.2 fusion.287
  358.5 8.1 %fusion.290 = f32[2,64,64,64]{3,2,1,0:T(8,128)S(1)} fusion(f32[2,64,64,128]{3,2,1,0:T(8,128)S(1)} %fusion.287), kind=kOutput, calls=%fused_computation.11.clone.1 | convolution fusion | flops 402710528 | bytes 6291456 | tf_op jit(solution)/shard_map/while/body/eval_jaxpr/exyk,yq->exqk/dot_general | solution.py:50
  366.6 23.1 %subtract_bitcast_fusion.4 = f32[2,64,64,64]{2,3,1,0:T(8,128)} fusion(f32[2,64,64,64]{3,2,1,0:T(8,128)S(1)} %fusion.290, f32[2,64,64,128]{3,2,1,0:T(8,128)S(1)} %fusion.287), kind=kOutput, calls=%fused_computation.8.clone.1 | convolution fusion | flops 403759104 | bytes 8388608 | tf_op jit(solution)/shard_map/while/body/eval_jaxpr/exyk,yq->exqk/dot_general | solution.py:47
  395.3 7.0 fusion.291
  402.3 8.0 %fusion.288 = f32[2,64,64,64]{3,2,1,0:T(8,128)S(1)} fusion(f32[2,64,64,128]{3,2,1,0:T(8,128)S(1)} %copy-done.5), kind=kOutput, calls=%fused_computation.9.clone.1 | convolution fusion | flops 402710528 | bytes 6291456 | tf_op jit(solution)/shard_map/while/body/eval_jaxpr/exyk,yq->exqk/dot_general | solution.py:49
  410.3 8.7 %add_bitcast_fusion.4 = f32[2,64,64,64]{2,3,1,0:T(8,128)} fusion(f32[2,64,64,64]{3,2,1,0:T(8,128)S(1)} %fusion.288, f32[2,64,64,128]{3,2,1,0:T(8,128)S(1)} %copy-done.5), kind=kOutput, calls=%fused_computation.7.clone.1 | convolution fusion | flops 403759104 | bytes 8388608 | tf_op jit(solution)/shard_map/while/body/eval_jaxpr/exyk,yq->exqk/dot_general | solution.py:48
  424.7 8.2 %subtract_bitcast_fusion.5 = f32[2,64,64,64]{1,3,2,0:T(8,128)S(1)} fusion(f32[2,64,64,64]{3,2,1,0:T(8,128)} %fusion.291, f32[2,64,64,64]{1,3,2,0:T(8,128)} %copy.109), kind=kOutput, calls=%fused_computation.6.clone.1 | convolution fusion | flops 403759104 | bytes 6291456 | tf_op jit(solution)/shard_map/while/body/eval_jaxpr/exqk,xr->erqk/dot_general | solution.py:50
  481.9 6.2 fusion.287
  488.0 8.1 %fusion.290 = f32[2,64,64,64]{3,2,1,0:T(8,128)S(1)} fusion(f32[2,64,64,128]{3,2,1,0:T(8,128)S(1)} %fusion.287), kind=kOutput, calls=%fused_computation.11.clone.1 | convolution fusion | flops 402710528 | bytes 6291456 | tf_op jit(solution)/shard_map/while/body/eval_jaxpr/exyk,yq->exqk/dot_general | solution.py:50
  496.2 23.1 %subtract_bitcast_fusion.4 = f32[2,64,64,64]{2,3,1,0:T(8,128)} fusion(f32[2,64,64,64]{3,2,1,0:T(8,128)S(1)} %fusion.290, f32[2,64,64,128]{3,2,1,0:T(8,128)S(1)} %fusion.287), kind=kOutput, calls=%fused_computation.8.clone.1 | convolution fusion | flops 403759104 | bytes 8388608 | tf_op jit(solution)/shard_map/while/body/eval_jaxpr/exyk,yq->exqk/dot_general | solution.py:47
  524.8 7.0 fusion.291
  531.9 8.0 %fusion.288 = f32[2,64,64,64]{3,2,1,0:T(8,128)S(1)} fusion(f32[2,64,64,128]{3,2,1,0:T(8,128)S(1)} %copy-done.5), kind=kOutput, calls=%fused_computation.9.clone.1 | convolution fusion | flops 402710528 | bytes 6291456 | tf_op jit(solution)/shard_map/while/body/eval_jaxpr/exyk,yq->exqk/dot_general | solution.py:49
  539.9 8.7 %add_bitcast_fusion.4 = f32[2,64,64,64]{2,3,1,0:T(8,128)} fusion(f32[2,64,64,64]{3,2,1,0:T(8,128)S(1)} %fusion.288, f32[2,64,64,128]{3,2,1,0:T(8,128)S(1)} %copy-done.5), kind=kOutput, calls=%fused_computation.7.clone.1 | convolution fusion | flops 403759104 | bytes 8388608 | tf_op jit(solution)/shard_map/while/body/eval_jaxpr/exyk,yq->exqk/dot_general | solution.py:48
  554.2 8.2 %subtract_bitcast_fusion.5 = f32[2,64,64,64]{1,3,2,0:T(8,128)S(1)} fusion(f32[2,64,64,64]{3,2,1,0:T(8,128)} %fusion.291, f32[2,64,64,64]{1,3,2,0:T(8,128)} %copy.109), kind=kOutput, calls=%fused_computation.6.clone.1 | convolution fusion | flops 403759104 | bytes 6291456 | tf_op jit(solution)/shard_map/while/body/eval_jaxpr/exqk,xr->erqk/dot_general | solution.py:50
  617.6 8.1 %fusion.290 = f32[2,64,64,64]{3,2,1,0:T(8,128)S(1)} fusion(f32[2,64,64,128]{3,2,1,0:T(8,128)S(1)} %fusion.287), kind=kOutput, calls=%fused_computation.11.clone.1 | convolution fusion | flops 402710528 | bytes 6291456 | tf_op jit(solution)/shard_map/while/body/eval_jaxpr/exyk,yq->exqk/dot_general | solution.py:50
  625.7 23.1 %subtract_bitcast_fusion.4 = f32[2,64,64,64]{2,3,1,0:T(8,128)} fusion(f32[2,64,64,64]{3,2,1,0:T(8,128)S(1)} %fusion.290, f32[2,64,64,128]{3,2,1,0:T(8,128)S(1)} %fusion.287), kind=kOutput, calls=%fused_computation.8.clone.1 | convolution fusion | flops 403759104 | bytes 8388608 | tf_op jit(solution)/shard_map/while/body/eval_jaxpr/exyk,yq->exqk/dot_general | solution.py:47
  654.4 7.0 fusion.291
  661.4 8.0 %fusion.288 = f32[2,64,64,64]{3,2,1,0:T(8,128)S(1)} fusion(f32[2,64,64,128]{3,2,1,0:T(8,128)S(1)} %copy-done.5), kind=kOutput, calls=%fused_computation.9.clone.1 | convolution fusion | flops 402710528 | bytes 6291456 | tf_op jit(solution)/shard_map/while/body/eval_jaxpr/exyk,yq->exqk/dot_general | solution.py:49
  669.4 8.7 %add_bitcast_fusion.4 = f32[2,64,64,64]{2,3,1,0:T(8,128)} fusion(f32[2,64,64,64]{3,2,1,0:T(8,128)S(1)} %fusion.288, f32[2,64,64,128]{3,2,1,0:T(8,128)S(1)} %copy-done.5), kind=kOutput, calls=%fused_computation.7.clone.1 | convolution fusion | flops 403759104 | bytes 8388608 | tf_op jit(solution)/shard_map/while/body/eval_jaxpr/exyk,yq->exqk/dot_general | solution.py:48
  683.8 8.2 %subtract_bitcast_fusion.5 = f32[2,64,64,64]{1,3,2,0:T(8,128)S(1)} fusion(f32[2,64,64,64]{3,2,1,0:T(8,128)} %fusion.291, f32[2,64,64,64]{1,3,2,0:T(8,128)} %copy.109), kind=kOutput, calls=%fused_computation.6.clone.1 | convolution fusion | flops 403759104 | bytes 6291456 | tf_op jit(solution)/shard_map/while/body/eval_jaxpr/exqk,xr->erqk/dot_general | solution.py:50
  (201 shorter events, 254.6 us)
Async XLA Ops:
  6.2 5.9 copy-start.2
  6.2 5.9 copy-start.3
  121.8 85.5 %copy-start = (f32[2,1024,128]{2,1,0:T(8,128)}, f32[2,1024,128]{2,1,0:T(8,128)S(1)}, u32[]{:S(2)}) copy-start(f32[2,1024,128]{2,1,0:T(8,128)S(1)} %sweeps.1) | copy-start | bytes 3145732
  121.8 45.1 %copy-start.8 = (s32[1,1,4]{2,1,0:T(1,128)S(1)}, s32[1,1,4]{2,1,0:T(1,128)}, u32[]{:S(2)}) copy-start(s32[1,1,4]{2,1,0:T(1,128)} %param.17) | copy-start | bytes 52
  121.8 45.1 %copy-start.9 = (s32[1,1,4]{2,1,0:T(1,128)S(1)}, s32[1,1,4]{2,1,0:T(1,128)}, u32[]{:S(2)}) copy-start(s32[1,1,4]{2,1,0:T(1,128)} %param.16) | copy-start | bytes 52
  121.8 45.1 %copy-start.10 = (s32[1,1,4]{2,1,0:T(1,128)S(1)}, s32[1,1,4]{2,1,0:T(1,128)}, u32[]{:S(2)}) copy-start(s32[1,1,4]{2,1,0:T(1,128)} %param.15) | copy-start | bytes 52
  121.8 17.0 %collective-permute-start.1 = (f32[2,32,32,128]{3,2,1,0:T(8,128)S(1)}, f32[2,32,32,128]{3,2,1,0:T(8,128)S(1)}, u32[]{:S(2)}, u32[]{:S(2)}) collective-permute-start(f32[2,32,32,128]{3,2,1,0:T(8,128)S(1)} %bitcast.169), channel_id=1, source_target_pairs={{8,0},{16,8},{24,16},{32,24},{40,32},{48,40},{56,48},{64,56},{72,6... | collective-permute-start | bytes 3145736 | tf_op jit(solution)/shard_map/ppermute | solution.py:28
  125.6 18.1 %collective-permute-start = (f32[2,32,32,128]{3,2,1,0:T(8,128)S(1)}, f32[2,32,32,128]{3,2,1,0:T(8,128)S(1)}, u32[]{:S(2)}, u32[]{:S(2)}) collective-permute-start(f32[2,32,32,128]{3,2,1,0:T(8,128)S(1)} %bitcast.170), channel_id=1, source_target_pairs={{0,8},{8,16},{16,24},{24,32},{32,40},{40,48},{48,56},{56,64},{64,7... | collective-permute-start | bytes 3145736 | tf_op jit(solution)/shard_map/ppermute | solution.py:25
  145.7 54.5 %collective-permute-start.3 = (f32[2,96,32,128]{3,2,1,0:T(8,128)}, f32[2,96,32,128]{3,2,1,0:T(8,128)}, u32[]{:S(2)}, u32[]{:S(2)}) collective-permute-start(f32[2,96,32,128]{3,2,1,0:T(8,128)} %pad_maximum_fusion.1), channel_id=1, source_target_pairs={{1,0},{2,1},{3,2},{4,3},{5,4},{6,5},{7,6},{9,8},{10,9},{11,10},{12... | collective-permute-start | bytes 9437192 | tf_op jit(solution)/shard_map/ppermute | solution.py:28
  163.5 37.9 %collective-permute-start.2 = (f32[2,96,32,128]{3,2,1,0:T(8,128)}, f32[2,96,32,128]{3,2,1,0:T(8,128)}, u32[]{:S(2)}, u32[]{:S(2)}) collective-permute-start(f32[2,96,32,128]{3,2,1,0:T(8,128)} %pad_maximum_fusion.1), channel_id=1, source_target_pairs={{0,1},{1,2},{2,3},{3,4},{4,5},{5,6},{6,7},{8,9},{9,10},{10,11},{11... | collective-permute-start | bytes 9437192 | tf_op jit(solution)/shard_map/ppermute | solution.py:25
  207.3 519.4 %copy-start.1 = (f32[2,1024,128]{2,1,0:T(8,128)S(1)}, f32[2,1024,128]{2,1,0:T(8,128)}, u32[]{:S(2)}) copy-start(f32[2,1024,128]{2,1,0:T(8,128)} %copy-done) | copy-start | bytes 3145732
  228.8 8.1 %copy-start.4 = (f32[2,64,64,128]{3,2,1,0:T(8,128)}, f32[2,64,64,128]{3,2,1,0:T(8,128)S(1)}, u32[]{:S(2)}) copy-start(f32[2,64,64,128]{3,2,1,0:T(8,128)S(1)} %fusion.287) | copy-start | bytes 12582916 | tf_op jit(solution)/shard_map/while
  265.7 7.0 copy-start.5
  295.1 8.2 %copy-start.7 = (f32[2,64,64,64]{1,3,2,0:T(8,128)S(1)}, f32[2,64,64,64]{1,3,2,0:T(8,128)}, u32[]{:S(2)}) copy-start(f32[2,64,64,64]{1,3,2,0:T(8,128)} %copy.109) | copy-start | bytes 6291460 | tf_op jit(solution)/shard_map/while
  303.4 3.8 copy-start.6
  358.5 8.1 %copy-start.4 = (f32[2,64,64,128]{3,2,1,0:T(8,128)}, f32[2,64,64,128]{3,2,1,0:T(8,128)S(1)}, u32[]{:S(2)}) copy-start(f32[2,64,64,128]{3,2,1,0:T(8,128)S(1)} %fusion.287) | copy-start | bytes 12582916 | tf_op jit(solution)/shard_map/while
  395.3 7.0 copy-start.5
  424.7 8.2 %copy-start.7 = (f32[2,64,64,64]{1,3,2,0:T(8,128)S(1)}, f32[2,64,64,64]{1,3,2,0:T(8,128)}, u32[]{:S(2)}) copy-start(f32[2,64,64,64]{1,3,2,0:T(8,128)} %copy.109) | copy-start | bytes 6291460 | tf_op jit(solution)/shard_map/while
  432.9 3.8 copy-start.6
  488.0 8.1 %copy-start.4 = (f32[2,64,64,128]{3,2,1,0:T(8,128)}, f32[2,64,64,128]{3,2,1,0:T(8,128)S(1)}, u32[]{:S(2)}) copy-start(f32[2,64,64,128]{3,2,1,0:T(8,128)S(1)} %fusion.287) | copy-start | bytes 12582916 | tf_op jit(solution)/shard_map/while
  524.8 7.0 copy-start.5
  554.2 8.2 %copy-start.7 = (f32[2,64,64,64]{1,3,2,0:T(8,128)S(1)}, f32[2,64,64,64]{1,3,2,0:T(8,128)}, u32[]{:S(2)}) copy-start(f32[2,64,64,64]{1,3,2,0:T(8,128)} %copy.109) | copy-start | bytes 6291460 | tf_op jit(solution)/shard_map/while
  562.5 3.8 copy-start.6
  617.6 8.1 %copy-start.4 = (f32[2,64,64,128]{3,2,1,0:T(8,128)}, f32[2,64,64,128]{3,2,1,0:T(8,128)S(1)}, u32[]{:S(2)}) copy-start(f32[2,64,64,128]{3,2,1,0:T(8,128)S(1)} %fusion.287) | copy-start | bytes 12582916 | tf_op jit(solution)/shard_map/while
  654.4 7.0 copy-start.5
  683.8 8.2 %copy-start.7 = (f32[2,64,64,64]{1,3,2,0:T(8,128)S(1)}, f32[2,64,64,64]{1,3,2,0:T(8,128)}, u32[]{:S(2)}) copy-start(f32[2,64,64,64]{1,3,2,0:T(8,128)} %copy.109) | copy-start | bytes 6291460 | tf_op jit(solution)/shard_map/while
  692.0 3.8 copy-start.6
  726.6 1.0 copy-start.11

commit v2 on v1

--- a/solution.py
+++ b/solution.py
@@ -1,8 +1,7 @@
-import functools
-import math
-
 import jax
 import jax.numpy as jnp
+import ml_dtypes
+import numpy as np
 from jax import lax
 from jax.experimental import pallas as pl
 from jax.experimental.pallas import tpu as pltpu
@@ -15,6 +14,8 @@
 WIN = 64
 DISP = 16
 SWEEPS = 2
+SPAN = 80
+KEPT = 40
 
 
 def padded_2(block, sides, width):
@@ -28,59 +29,6 @@
         high = lax.ppermute(lax.slice_in_dim(block, 0, width, axis=dim), axis, backward)
         block = jnp.concatenate([low, block, high], axis=dim)
     return block
-
-
-def dft_tables():
-    indices = jnp.arange(WIN, dtype=jnp.int32)
-    full_angle = (
-        2.0 * math.pi / WIN * (indices[:, None] * indices[None, :] % WIN).astype(jnp.float32)
-    )
-    shifts = (jnp.arange(DISP, dtype=jnp.int32) - DISP // 2) % WIN
-    part_angle = (
-        2.0 * math.pi / WIN * (indices[:, None] * shifts[None, :] % WIN).astype(jnp.float32)
-    )
-    return (jnp.cos(full_angle), jnp.sin(full_angle), jnp.cos(part_angle), jnp.sin(part_angle))
-
-
-def turn_axis(real_part, imag_part, cosine, sine_table, form, sign):
-    highest = lax.Precision.HIGHEST
-    real_cos = jnp.einsum(form, real_part, cosine, precision=highest)
-    real_sin = jnp.einsum(form, real_part, sine_table, precision=highest)
-    imag_cos = jnp.einsum(form, imag_part, cosine, precision=highest)
-    imag_sin = jnp.einsum(form, imag_part, sine_table, precision=highest)
-    return (real_cos - sign * imag_sin, imag_cos + sign * real_sin)
-
-
-def window_correlation(extended, start, tables):
-    cosine, sine_table, cos_part, sin_part = tables
-    highest = lax.Precision.HIGHEST
-    window = lax.dynamic_slice(
-        extended, (jnp.int32(0), start[0], start[1], start[2]), (2, WIN, WIN, WIN)
-    )
-    centred = window - jnp.mean(window, axis=(1, 2, 3), keepdims=True)
-    rms = jnp.sqrt(jnp.mean(centred * centred, axis=(1, 2, 3)) + 1e-06)
-    stacked = jnp.concatenate([cosine, -sine_table], axis=1)
-    first = jnp.einsum("exyz,zk->exyk", centred, stacked, precision=highest)
-    real_part = first[..., :WIN]
-    imag_part = first[..., WIN:]
-    real_part, imag_part = turn_axis(
-        real_part, imag_part, cosine, sine_table, "exyk,yq->exqk", -1.0
-    )
-    real_part, imag_part = turn_axis(
-        real_part, imag_part, cosine, sine_table, "exqk,xr->erqk", -1.0
-    )
-    cross_real = real_part[0] * real_part[1] + imag_part[0] * imag_part[1]
-    cross_imag = real_part[0] * imag_part[1] - imag_part[0] * real_part[1]
-    cross_real, cross_imag = turn_axis(
-        cross_real, cross_imag, cos_part, sin_part, "abk,kd->abd", 1.0
-    )
-    cross_real, cross_imag = turn_axis(
-        cross_real, cross_imag, cos_part, sin_part, "abd,bq->aqd", 1.0
-    )
-    final = jnp.einsum("aqd,ar->rqd", cross_real, cos_part, precision=highest)
-    final = final - jnp.einsum("aqd,ar->rqd", cross_imag, sin_part, precision=highest)
-    scale = 1.0 / (WIN**3 * WIN**1.5)
-    return (final * scale / (rms[0] * rms[1])).reshape(-1)
 
 
 def sweeps_kernel(
@@ -305,18 +253,233 @@
     ).reshape(initial.shape)
 
 
+def split(values):
+    high = values.astype(jnp.bfloat16)
+    return high, (values - high.astype(jnp.float32)).astype(jnp.bfloat16)
+
+
+def window_tables():
+    bf16 = ml_dtypes.bfloat16
+    turn = 2.0 * np.pi / WIN
+
+    def parts(table):
+        high = table.astype(bf16)
+        return high, (table - high.astype(np.float64)).astype(bf16)
+
+    waves = np.arange(WIN // 2 + 1)
+    angle = turn * (waves[:, None] * np.arange(SPAN)[None, :] % WIN)
+    left = np.zeros((2 * KEPT, SPAN))
+    left[: len(waves)] = np.cos(angle)
+    left[KEPT : KEPT + len(waves)] = -np.sin(angle)
+    left_high, left_low = parts(left)
+    left_table = np.zeros((2 * KEPT, 256), bf16)
+    for place, table in enumerate((left_high, left_high, left_low)):
+        left_table[:, place * SPAN : (place + 1) * SPAN] = table
+
+    angle = turn * (np.arange(128)[:, None] * np.arange(WIN)[None, :] % WIN)
+    cosine, sine = np.cos(angle), np.sin(angle)
+    right = np.block([[cosine, -sine, -sine, cosine], [sine, cosine, cosine, sine]])
+    right_table = np.stack(parts(right))
+
+    shifts = np.arange(DISP) - DISP // 2
+    weight = np.where(waves % (WIN // 2) == 0, 1.0, 2.0)
+    angle = turn * shifts[:, None] * waves[None, :]
+    inverse_left = np.zeros((2 * DISP, KEPT))
+    inverse_left[:DISP, : len(waves)] = weight * np.cos(angle)
+    inverse_left[DISP:, : len(waves)] = weight * np.sin(angle)
+    angle = turn * np.arange(WIN)[:, None] * shifts[None, :]
+    cosine, sine = np.cos(angle), np.sin(angle)
+    inverse_right = np.zeros((512, 128))
+    inverse_right[:, :DISP] = np.concatenate(
+        [cosine, cosine, -sine, sine, -sine, -sine, -cosine, cosine]
+    )
+    row_weight = np.zeros((KEPT, 128))
+    row_weight[: len(waves)] = weight[:, None]
+    f32 = np.float32
+    return (
+        left_table, right_table,
+        inverse_left.astype(f32), inverse_right.astype(f32), row_weight.astype(f32),
+    )
+
+
+def windows_kernel(
+    place_ref, ext_ref, left_ref, right_ref, inv_left_ref, inv_right_ref, weight_ref,
+    out_ref,
+    high_ref, low_ref, mid_high, mid_low, spec0, spec1, corr_ref,
+):
+    f32 = jnp.float32
+    half = DISP // 2
+    wide_x = ext_ref.shape[1]
+    brick = wide_x // 3
+
+    def whole_sum(values):
+        return jnp.sum(jnp.sum(values, axis=0, keepdims=True), axis=1, keepdims=True)
+
+    for e in range(2):
+        def add(x, total):
+            return total + ext_ref[e, brick + x, brick : 2 * brick, :]
+
+        total = lax.fori_loop(0, brick, add, jnp.zeros((brick, 128), f32), unroll=4)
+        offset = whole_sum(total) * (1.0 / (brick * brick * 128))
+
+        def part(x, _):
+            high, low = split(ext_ref[e, x] - offset)
+            high_ref[e, x] = high
+            low_ref[e, x] = low
+            return 0
+
+        lax.fori_loop(0, wide_x, part, 0, unroll=2)
+
+    def one_window(w, _):
+        start_x, start_y, start_z = place_ref[0, w], place_ref[1, w], place_ref[2, w]
+        from_y = pl.multiple_of(start_y // 16 * 16, 16)
+        lead = start_y - from_y
+        lane = lax.broadcasted_iota(jnp.int32, (2 * KEPT, 256), 1)
+        spot = lax.rem(lane, SPAN)
+        keep = (spot >= lead) & (spot < lead + WIN) & (lane < 3 * SPAN)
+        left = jnp.where(keep, left_ref[...].astype(f32), 0.0).astype(jnp.bfloat16)
+        row = lax.rem(lax.broadcasted_iota(jnp.int32, (256, 256), 0), 128)
+        keep = (row >= start_z) & (row < start_z + WIN)
+        right_high = jnp.where(keep, right_ref[0].astype(f32), 0.0).astype(jnp.bfloat16)
+        right_low = jnp.where(keep, right_ref[1].astype(f32), 0.0).astype(jnp.bfloat16)
+
+        def turn_y(x, _):
+            rows = pl.ds(from_y, SPAN)
+            sides = []
+            for e in range(2):
+                high = high_ref[e, start_x + x, rows, :]
+                low = low_ref[e, start_x + x, rows, :]
+                sides.append(jnp.concatenate([high, low, high, high[0:16]], axis=0))
+            mixed = jnp.dot(left, jnp.concatenate(sides, axis=1), preferred_element_type=f32)
+            high, low = split(mixed)
+            for e in range(2):
+                lanes = slice(e * 128, (e + 1) * 128)
+                for source, target in ((high, mid_high), (low, mid_low)):
+                    target[e, x, :, 0:128] = source[0:KEPT, lanes]
+                    target[e, x, :, 128:256] = source[KEPT : 2 * KEPT, lanes]
+            return 0
+
+        lax.fori_loop(0, WIN, turn_y, 0, unroll=4)
+
+        def turn_z(i, _):
+            xs = pl.ds(i * 16, 16)
+            for e in range(2):
+                lanes = slice(0, 128 * (e + 1))
+                high = mid_high[e, xs].reshape(16 * KEPT, 256)
+                low = mid_low[e, xs].reshape(16 * KEPT, 256)
+                value = jnp.dot(high, right_high[:, lanes], preferred_element_type=f32)
+                value += jnp.dot(low, right_high[:, lanes], preferred_element_type=f32)
+                value += jnp.dot(high, right_low[:, lanes], preferred_element_type=f32)
+                if e == 0:
+                    spec0[xs] = value.reshape(16, KEPT, 128)
+                else:
+                    spec1[pl.ds(i * 16 + half, 16)] = value.reshape(16, KEPT, 256)
+            return 0
+
+        lax.fori_loop(0, WIN // 16, turn_z, 0)
+
+        def sums(x, carry):
+            return carry[0] + spec0[x, 0:8, :], carry[1] + spec1[x + half, 0:8, :]
+
+        mean0, mean1 = lax.fori_loop(
+            0, WIN, sums, (jnp.zeros((8, 128), f32), jnp.zeros((8, 256), f32)), unroll=4
+        )
+        lane = lax.broadcasted_iota(jnp.int32, (8, 256), 1)
+        row = lax.broadcasted_iota(jnp.int32, (8, 256), 0)
+        mean1 = jnp.where((row == 0) & ((lane == 0) | (lane == 192)), mean1 * (1.0 / WIN), 0.0)
+        mean0 = jnp.where((row == 0) & (lane == 0), mean0_wide(mean0), 0.0)[:, 0:128]
+
+        def centre(x, carry):
+            spec0[x, 0:8, :] = spec0[x, 0:8, :] - mean0
+            spec1[x + half, 0:8, :] = spec1[x + half, 0:8, :] - mean1
+            value0, value1 = spec0[x], spec1[x + half, :, 0:128]
+            return carry[0] + value0 * value0, carry[1] + value1 * value1
+
+        zero = jnp.zeros((KEPT, 128), f32)
+        power0, power1 = lax.fori_loop(0, WIN, centre, (zero, zero), unroll=2)
+        count = 1.0 / (WIN * WIN * WIN**3)
+        rms0 = jnp.sqrt(whole_sum(power0 * weight_ref[...]) * count + 1e-6)
+        rms1 = jnp.sqrt(whole_sum(power1 * weight_ref[...]) * count + 1e-6)
+        spec1[0:half] = spec1[WIN : WIN + half]
+        spec1[WIN + half : WIN + DISP] = spec1[half:DISP]
+
+        def group(g, _):
+            rows = pl.ds(pl.multiple_of(lax.rem(g, KEPT // 8) * 8, 8), 8)
+            first = lax.div(g, KEPT // 8) * half
+
+            def block(i, carry):
+                carry = list(carry)
+                base = i * 4
+                ones = [spec0[base + j, rows, :] for j in range(4)]
+                plain = [spec1[base + first + j, rows, 0:128] for j in range(half + 3)]
+                swapped = [spec1[base + first + j, rows, 128:256] for j in range(half + 3)]
+                for j in range(4):
+                    for s in range(half):
+                        carry[s] = carry[s] + ones[j] * plain[j + s]
+                        carry[half + s] = carry[half + s] + ones[j] * swapped[j + s]
+                return tuple(carry)
+
+            zero = jnp.zeros((8, 128), f32)
+            done = lax.fori_loop(0, WIN // 4, block, (zero,) * DISP)
+            for s in range(half):
+                corr_ref[first + s, rows, 0:128] = done[s]
+                corr_ref[first + s, rows, 128:256] = done[half + s]
+            return 0
+
+        lax.fori_loop(0, 2 * (KEPT // 8), group, 0)
+
+        highest = lax.Precision.HIGHEST
+        turned = []
+        for s in range(DISP):
+            value = jnp.dot(
+                inv_left_ref[...], corr_ref[s], precision=highest, preferred_element_type=f32
+            )
+            turned.append(jnp.concatenate([value[0:DISP], value[DISP : 2 * DISP]], axis=1))
+        final = jnp.dot(
+            jnp.concatenate(turned, axis=0), inv_right_ref[...],
+            precision=highest, preferred_element_type=f32,
+        )
+        scale = 1.0 / (WIN * WIN * WIN**1.5)
+        out_ref[w] = (final * (scale / (rms0 * rms1)))[:, 0:DISP]
+        return 0
+
+    lax.fori_loop(0, out_ref.shape[0], one_window, 0)
+
+
+def mean0_wide(values):
+    return jnp.concatenate([values, values], axis=1) * (1.0 / WIN)
+
+
+def correlate(extended, win_x, win_y, win_z):
+    windows = win_x.size
+    places = jnp.stack([win_x.reshape(-1), win_y.reshape(-1), win_z.reshape(-1)])
+    vmem = pl.BlockSpec(memory_space=pltpu.VMEM)
+    bf16 = jnp.bfloat16
+    shape = extended.shape
+    return pl.pallas_call(
+        windows_kernel,
+        out_shape=jax.ShapeDtypeStruct((windows, DISP * DISP, DISP), jnp.float32),
+        in_specs=[pl.BlockSpec(memory_space=pltpu.SMEM)] + [vmem] * 6,
+        out_specs=vmem,
+        scratch_shapes=[
+            pltpu.VMEM(shape, bf16),
+            pltpu.VMEM(shape, bf16),
+            pltpu.VMEM((2, WIN, KEPT, 256), bf16),
+            pltpu.VMEM((2, WIN, KEPT, 256), bf16),
+            pltpu.VMEM((WIN, KEPT, 128), jnp.float32),
+            pltpu.VMEM((WIN + DISP, KEPT, 256), jnp.float32),
+            pltpu.VMEM((DISP, KEPT, 256), jnp.float32),
+        ],
+        compiler_params=pltpu.CompilerParams(vmem_limit_bytes=56 * 1024 * 1024),
+        name="windows",
+    )(places, extended, *[jnp.asarray(table) for table in window_tables()])
+
+
 def body(initial, images, blocks, lib_index, tile_map, win_x, win_y, win_z):
     volume = reconstruct(initial, images, blocks, lib_index, tile_map)
     extended = padded_2(volume, (("wide", 1), ("narrow", 2)), WIN // 2)
-    tables = dft_tables()
-    starts = jnp.stack([win_x.reshape(-1), win_y.reshape(-1), win_z.reshape(-1)], axis=1)
-
-    def per_window(start):
-        return window_correlation(extended, start, tables)
-
-    results = lax.map(per_window, starts)
-    correlation = results.reshape(1, 1, starts.shape[0], DISP * DISP * DISP)
-    return (volume, correlation)
+    correlation = correlate(extended, win_x, win_y, win_z)
+    return (volume, correlation.reshape(1, 1, win_x.size, DISP * DISP * DISP))
 
 
 def solution(mesh):

time: 738 us -> 262 us (0.36); the launches traced: 728 us -> 259 us
  matrix products: 367 us -> 0 us
  local copies, waits for them, and re-layouts: 84.8 us -> 5.87 us
  Pallas kernels: 110 us -> 164 us
  other arithmetic: 58.5 us -> 12 us
  loops' own time: 29.3 us -> 0 us
    dot_general x76 -> x0, matrix products: 367 us -> none  [the longest x16 135 us: turn_axis(): real_cos = jnp.einsum(form, real_part, cosine, precision=highest)]
    pallas_call x0 -> x1, Pallas kernels: none -> 54 us  [correlate(): pl.pallas_call(windows_kernel, out_shape=jax.ShapeDtypeStruct((windows, D...]
    ppermute x2, waiting for transfers between devices: 44.2 us -> 5.1 us  [padded_2(): lax.ppermute(lax.slice_in_dim(block, 0, width, axis=dim), axis, backward)]
    ppermute x2, waiting for transfers between devices: 6.11 us -> 42.7 us  [padded_2(): lax.ppermute(lax.slice_in_dim(block, block.shape[dim] - width, None, axis...]
    another operation x1 -> x0, loops' own time: 29.3 us -> none  [body(): results = lax.map(per_window, starts)]
    reduce_sum x8 -> x0, other arithmetic: 28.8 us -> none  [the longest x4 14.4 us: window_correlation(): centred = window - jnp.mean(window, axis=(1, 2, 3), keepdims=True)]
    dot_general x16 -> x0, local copies, waits for them, and re-layouts: 28.4 us -> none  [the longest x4 8.69 us: turn_axis(): imag_sin = jnp.einsum(form, imag_part, sine_table, precision=highest)]
    add x4 -> x0, local copies, waits for them, and re-layouts: 22.6 us -> none  [turn_axis(): return (real_cos - sign * imag_sin, imag_cos + sign * real_sin)]
where the time goes in v2:
time: 262 us; the launch traced here: 259 us
  Pallas kernels  164 us (63%)
  waiting for transfers between devices  47.8 us (18%)
  starting transfers between devices  29.3 us (11%)
  other arithmetic  12 us (5%)
  local copies, waits for them, and re-layouts  5.87 us (2%)
    pallas_call x1, Pallas kernels, reconstruct(): pl.pallas_call(sweeps_kernel, out_shape=jax.ShapeDtypeStruct((2, columns,...  110 us
    pallas_call x1, Pallas kernels, correlate(): pl.pallas_call(windows_kernel, out_shape=jax.ShapeDtypeStruct((windows, D...  54 us
    ppermute x2, waiting for transfers between devices, padded_2(): lax.ppermute(lax.slice_in_dim(block, block.shape[dim] - width, None, axis...  42.7 us
    ppermute x2, starting transfers between devices, padded_2(): lax.ppermute(lax.slice_in_dim(block, block.shape[dim] - width, None, axis...  22.3 us
    ppermute x2, starting transfers between devices, padded_2(): lax.ppermute(lax.slice_in_dim(block, 0, width, axis=dim), axis, backward)  7.07 us
  transfers between devices with their start and end apart: 4, of which 4 were waited for; matrix products, arithmetic and copies ran while one was open for 0% of the time, Pallas kernels for 0%

profile of v2, /device:TPU:9, one launch (start us, length us, event | category | flops | bytes accessed | tf_op | source)
XLA Modules:
  0.0 259.4 jit_solution(338009481469039647)
XLA Ops:
  0.6 1.0 broadcast_divide_fusion
  1.6 0.9 sign_compare_fusion
  2.5 0.1 div.18
  2.6 0.1 rem.31
  2.7 0.1 ne.56
  2.8 0.0 copy-start.2
  2.8 2.4 fusion.spread_ref
  5.2 2.9 %fusion.1.gather_ref = bf16[4,384,1024]{2,1,0:T(8,128)(2,1)} fusion(s32[4,1024]{1,0:T(4,128)S(1)} %get-tuple-element.5), kind=kLoop, calls=%fused_computation.4 | loop fusion | flops 3145728 | bytes 3162112 | tf_op jit(solution)/shard_map/convert_element_type | solution.py:251
  8.1 0.0 copy-done.3
  8.1 0.1 convert_element_type.14
  8.2 0.7 copy.18
  8.9 0.6 broadcast_in_dim.5.lib_ref
  9.6 0.0 copy-start.1
  9.6 1.2 copy-done.1
  10.8 109.6 %sweeps.1 = f32[2,1024,128]{2,1,0:T(8,128)S(1)} custom-call(f32[2,1024,128]{2,1,0:T(8,128)S(1)} %bitcast.17, f32[2,4,24,128]{3,2,1,0:T(8,128)S(1)} %pad.4.img_ref, bf16[4,1024,128]{2,1,0:T(8,128)(2,1)S(1)} %bitcast.16, bf16[4,1024,128]{2,1,0:T(8,128)(2,1)S(1)} %bitcast.15, bf16[4,1024,128]{2,1,0:T(8,128)(2,1)S(1)} %broadcast_in_dim.5.lib_ref, ...), custom_call_target="tpu_custom_call" | custom-call | tf_op jit(solution)/shard_map/sweeps/pallas_call | solution.py:226
  120.3 0.0 copy-start.4
  120.4 0.0 copy-start.5
  120.4 0.0 copy-start.6
  120.4 2.4 collective-permute-start
  122.8 5.2 %collective-permute-start.1 = (f32[2,32,32,128]{3,2,1,0:T(8,128)S(1)}, f32[2,32,32,128]{3,2,1,0:T(8,128)S(1)}, u32[]{:S(2)}, u32[]{:S(2)}) collective-permute-start(f32[2,32,32,128]{3,2,1,0:T(8,128)S(1)} %bitcast.10), channel_id=1, source_target_pairs={{8,0},{16,8},{24,16},{32,24},{40,32},{48,40},{56,48},{64,56},{72,6... | collective-permute-start | bytes 3145736 | tf_op jit(solution)/shard_map/ppermute | solution.py:29
  127.9 11.0 %collective-permute-done = f32[2,32,32,128]{3,2,1,0:T(8,128)S(1)} collective-permute-done((f32[2,32,32,128]{3,2,1,0:T(8,128)S(1)}, f32[2,32,32,128]{3,2,1,0:T(8,128)S(1)}, u32[]{:S(2)}, u32[]{:S(2)}) %collective-permute-start) | collective-permute-done | bytes 1048608 | tf_op jit(solution)/shard_map/ppermute | solution.py:26
  139.0 0.7 collective-permute-done.1
  139.7 0.3 pad_maximum_fusion.1
  140.0 19.9 %collective-permute-start.2 = (f32[2,96,32,128]{3,2,1,0:T(8,128)S(1)}, f32[2,96,32,128]{3,2,1,0:T(8,128)S(1)}, u32[]{:S(2)}, u32[]{:S(2)}) collective-permute-start(f32[2,96,32,128]{3,2,1,0:T(8,128)S(1)} %pad_maximum_fusion.1), channel_id=1, source_target_pairs={{0,1},{1,2},{2,3},{3,4},{4,5},{5,6},{6,7},{8,9},{9,10},{10,11},{11... | collective-permute-start | bytes 9437192 | tf_op jit(solution)/shard_map/ppermute | solution.py:26
  159.9 1.9 collective-permute-start.3
  161.8 0.6 pad_add_fusion.place_ref
  162.4 31.6 %collective-permute-done.2 = f32[2,96,32,128]{3,2,1,0:T(8,128)S(1)} collective-permute-done((f32[2,96,32,128]{3,2,1,0:T(8,128)S(1)}, f32[2,96,32,128]{3,2,1,0:T(8,128)S(1)}, u32[]{:S(2)}, u32[]{:S(2)}) %collective-permute-start.2) | collective-permute-done | bytes 3145760 | tf_op jit(solution)/shard_map/ppermute | solution.py:26
  194.1 4.4 %collective-permute-done.3 = f32[2,96,32,128]{3,2,1,0:T(8,128)S(1)} collective-permute-done((f32[2,96,32,128]{3,2,1,0:T(8,128)S(1)}, f32[2,96,32,128]{3,2,1,0:T(8,128)S(1)}, u32[]{:S(2)}, u32[]{:S(2)}) %collective-permute-start.3) | collective-permute-done | bytes 3145760 | tf_op jit(solution)/shard_map/ppermute | solution.py:29
  198.5 4.0 %pad_maximum_fusion.ext_ref = f32[2,96,96,128]{3,2,1,0:T(8,128)} fusion(f32[2,96,32,128]{3,2,1,0:T(8,128)S(1)} %collective-permute-done.3, f32[2,32,32,128]{3,2,1,0:T(8,128)S(1)} %collective-permute-done.1, f32[2,32,32,128]{3,2,1,0:T(8,128)S(1)} %bitcast.12, f32[2,32,32,128]{3,2,1,0:T(8,128)S(1)} %collective-permute-done, ...), kind=kLoop, calls=%fused_computation | loop fusion | flops 9437184 | bytes 18874368 | tf_op jit(solution)/shard_map/concatenate | solution.py:30
  202.4 54.0 %windows.1 = f32[4,256,16]{2,1,0:T(8,128)} custom-call(s32[3,4]{1,0:T(4,128)} %pad_add_fusion.place_ref, f32[2,96,96,128]{3,2,1,0:T(8,128)} %pad_maximum_fusion.ext_ref, bf16[80,256]{1,0:T(8,128)(2,1)} %constant.53.clone.left_ref, bf16[2,256,256]{2,1,0:T(8,128)(2,1)} %constant.54.clone.right_ref, f32[32,40]{1,0:T(8,128)} %constant.55.clone.inv_left_ref, ...), custom_call_target="tpu_custom_call" | custom-call | tf_op jit(solution)/shard_map/windows/pallas_call | solution.py:459
  256.5 2.0 reshape.96
  258.4 1.0 copy.20
  (11 shorter events, 0.1 us)
Async XLA Ops:
  0.6 7.5 %copy-start.3 = (s32[4,32,32]{2,1,0:T(8,128)S(1)}, s32[4,32,32]{2,1,0:T(8,128)}, u32[]{:S(2)}) copy-start(s32[4,32,32]{2,1,0:T(8,128)} %param.16) | copy-start | bytes 49156
  0.6 7.6 %copy-start = (bf16[4,8,128,128]{3,2,1,0:T(8,128)(2,1)S(1)}, bf16[4,8,128,128]{3,2,1,0:T(8,128)(2,1)}, u32[]{:S(2)}) copy-start(bf16[4,8,128,128]{3,2,1,0:T(8,128)(2,1)} %param.15) | copy-start | bytes 3145732
  2.8 6.1 %copy-start.2 = (f32[2,4,3,6,128]{4,1,3,2,0:T(4,128)S(1)}, f32[2,4,3,6,128]{4,1,3,2,0:T(4,128)}, u32[]{:S(2)}) copy-start(f32[2,4,3,6,128]{4,1,3,2,0:T(4,128)} %param.14) | copy-start | bytes 221188
  9.6 1.2 copy-start.1
  120.3 41.5 %copy-start.4 = (s32[1,1,4]{2,1,0:T(1,128)S(1)}, s32[1,1,4]{2,1,0:T(1,128)}, u32[]{:S(2)}) copy-start(s32[1,1,4]{2,1,0:T(1,128)} %param.20) | copy-start | bytes 52
  120.4 41.5 %copy-start.5 = (s32[1,1,4]{2,1,0:T(1,128)S(1)}, s32[1,1,4]{2,1,0:T(1,128)}, u32[]{:S(2)}) copy-start(s32[1,1,4]{2,1,0:T(1,128)} %param.19) | copy-start | bytes 52
  120.4 41.5 %copy-start.6 = (s32[1,1,4]{2,1,0:T(1,128)S(1)}, s32[1,1,4]{2,1,0:T(1,128)}, u32[]{:S(2)}) copy-start(s32[1,1,4]{2,1,0:T(1,128)} %param.18) | copy-start | bytes 52
  120.4 18.6 %collective-permute-start = (f32[2,32,32,128]{3,2,1,0:T(8,128)S(1)}, f32[2,32,32,128]{3,2,1,0:T(8,128)S(1)}, u32[]{:S(2)}, u32[]{:S(2)}) collective-permute-start(f32[2,32,32,128]{3,2,1,0:T(8,128)S(1)} %bitcast.9), channel_id=1, source_target_pairs={{0,8},{8,16},{16,24},{24,32},{32,40},{40,48},{48,56},{56,64},{64,7... | collective-permute-start | bytes 3145736 | tf_op jit(solution)/shard_map/ppermute | solution.py:26
  122.8 16.9 %collective-permute-start.1 = (f32[2,32,32,128]{3,2,1,0:T(8,128)S(1)}, f32[2,32,32,128]{3,2,1,0:T(8,128)S(1)}, u32[]{:S(2)}, u32[]{:S(2)}) collective-permute-start(f32[2,32,32,128]{3,2,1,0:T(8,128)S(1)} %bitcast.10), channel_id=1, source_target_pairs={{8,0},{16,8},{24,16},{32,24},{40,32},{48,40},{56,48},{64,56},{72,6... | collective-permute-start | bytes 3145736 | tf_op jit(solution)/shard_map/ppermute | solution.py:29
  140.0 54.1 %collective-permute-start.2 = (f32[2,96,32,128]{3,2,1,0:T(8,128)S(1)}, f32[2,96,32,128]{3,2,1,0:T(8,128)S(1)}, u32[]{:S(2)}, u32[]{:S(2)}) collective-permute-start(f32[2,96,32,128]{3,2,1,0:T(8,128)S(1)} %pad_maximum_fusion.1), channel_id=1, source_target_pairs={{0,1},{1,2},{2,3},{3,4},{4,5},{5,6},{6,7},{8,9},{9,10},{10,11},{11... | collective-permute-start | bytes 9437192 | tf_op jit(solution)/shard_map/ppermute | solution.py:26
  159.9 38.6 %collective-permute-start.3 = (f32[2,96,32,128]{3,2,1,0:T(8,128)S(1)}, f32[2,96,32,128]{3,2,1,0:T(8,128)S(1)}, u32[]{:S(2)}, u32[]{:S(2)}) collective-permute-start(f32[2,96,32,128]{3,2,1,0:T(8,128)S(1)} %pad_maximum_fusion.1), channel_id=1, source_target_pairs={{1,0},{2,1},{3,2},{4,3},{5,4},{6,5},{7,6},{9,8},{10,9},{11,10},{12... | collective-permute-start | bytes 9437192 | tf_op jit(solution)/shard_map/ppermute | solution.py:29

commit v3 on v1

v3 whole, which is shorter than its diff:
```python
import jax
import jax.numpy as jnp
import ml_dtypes
import numpy as np
from jax import lax
from jax.experimental import pallas as pl
from jax.experimental.pallas import tpu as pltpu
from jax.sharding import PartitionSpec as P

MESH = pl.DeviceIdType.MESH
PROJ_ROWS = 24
RATIO_ROWS = 32
CHUNK = 256
WIN = 64
DISP = 16
SWEEPS = 2
SPAN = 80
KEPT = 40
BRICK = 32
MARK = 16
STEPS = 65000.0


def split(values):
    high = values.astype(jnp.bfloat16)
    return high, (values - high.astype(jnp.float32)).astype(jnp.bfloat16)


def window_tables():
    bf16 = ml_dtypes.bfloat16
    turn = 2.0 * np.pi / WIN

    def parts(table):
        high = table.astype(bf16)
        return high, (table - high.astype(np.float64)).astype(bf16)

    waves = np.arange(WIN // 2 + 1)
    angle = turn * (waves[:, None] * np.arange(SPAN)[None, :] % WIN)
    left = np.zeros((2 * KEPT, SPAN))
    left[: len(waves)] = np.cos(angle)
    left[KEPT : KEPT + len(waves)] = -np.sin(angle)
    left_high, left_low = parts(left)
    left_table = np.zeros((2 * KEPT, 256), bf16)
    for place, table in enumerate((left_high, left_high, left_low)):
        left_table[:, place * SPAN : (place + 1) * SPAN] = table

    angle = turn * (np.arange(128)[:, None] * np.arange(WIN)[None, :] % WIN)
    cosine, sine = np.cos(angle), np.sin(angle)
    right = np.block([[cosine, -sine, -sine, cosine], [sine, cosine, cosine, sine]])
    right_table = np.stack(parts(right))

    shifts = np.arange(DISP) - DISP // 2
    weight = np.where(waves % (WIN // 2) == 0, 1.0, 2.0)
    angle = turn * shifts[:, None] * waves[None, :]
    inverse_left = np.zeros((2 * DISP, KEPT))
    inverse_left[:DISP, : len(waves)] = weight * np.cos(angle)
    inverse_left[DISP:, : len(waves)] = weight * np.sin(angle)
    angle = turn * np.arange(WIN)[:, None] * shifts[None, :]
    cosine, sine = np.cos(angle), np.sin(angle)
    inverse_right = np.zeros((512, 128))
    inverse_right[:, :DISP] = np.concatenate(
        [cosine, cosine, -sine, sine, -sine, -sine, -cosine, cosine]
    )
    row_weight = np.zeros((KEPT, 128))
    row_weight[: len(waves)] = weight[:, None]
    f32 = np.float32
    return (
        left_table, right_table,
        inverse_left.astype(f32), inverse_right.astype(f32), row_weight.astype(f32),
    )


def wrapped(index, count):
    return jnp.where(index >= count, index - count, index)


def whole(values, reduce):
    return reduce(reduce(values, axis=0, keepdims=True), axis=1, keepdims=True)


def chunks(rows, action, unroll):
    def step(i, carry):
        return action(pl.ds(pl.multiple_of(i * CHUNK, CHUNK), CHUNK), carry)

    return lambda init: lax.fori_loop(0, rows // CHUNK, step, init, unroll=unroll)


def reconstruct(refs, scratch, barrier_done, finish):
    init_ref, img_ref, fwd_ref, bwd_ref, lib_ref, gather_ref, spread_ref, vol_ref = refs
    cols_ref, part_ref, recv_ref, ratio_ref = scratch[:4]
    part_send, part_recv, ratio_send, ratio_recv = scratch[4:]
    f32, bf16 = jnp.float32, jnp.bfloat16
    count = lax.axis_size("wide")
    me = lax.axis_index("wide")
    cams = fwd_ref.shape[0]
    columns = init_ref.shape[1]

    def by_library(values, cam, rows, table):
        lib = lib_ref[cam, rows, :]
        zero = jnp.zeros_like(values)
        odd = (lib == 1) | (lib == 3) | (lib == 5) | (lib == 7)
        lhs = jnp.concatenate(
            [jnp.where(odd, zero, values), jnp.where(odd, values, zero)], axis=1
        )
        wide = jnp.dot(lhs, table, preferred_element_type=f32)
        pair = lib.astype(f32)
        low = jnp.where(pair < 2, wide[:, 0:128], wide[:, 128:256])
        high = jnp.where(pair < 6, wide[:, 256:384], wide[:, 384:512])
        return jnp.where(pair < 4, low, high)

    def project_rows(e, cam, rows, vol):
        proj = by_library(vol.astype(bf16), cam, rows, fwd_ref[cam])
        high, low = split(proj)
        cols_ref[e, rows, 0:128] = high
        cols_ref[e, rows, 128:256] = low

    def part_copy(e, d, owner):
        target = wrapped(me + d, count)
        return pltpu.make_async_remote_copy(
            src_ref=part_ref.at[e, target],
            dst_ref=recv_ref.at[e, owner],
            send_sem=part_send.at[e, d],
            recv_sem=part_recv.at[e, owner],
            device_id={"wide": target},
            device_id_type=MESH,
        )

    def strip(e, owner):
        return ratio_ref.at[e, pl.ds(pl.multiple_of(owner * RATIO_ROWS, RATIO_ROWS), RATIO_ROWS)]

    def ratio_copy(e, d, owner):
        return pltpu.make_async_remote_copy(
            src_ref=strip(e, me),
            dst_ref=strip(e, owner),
            send_sem=ratio_send.at[e, d],
            recv_sem=ratio_recv.at[e, owner],
            device_id={"wide": wrapped(me + d, count)},
            device_id_type=MESH,
        )

    def each(action):
        def step(d, _):
            action(d)
            return 0

        lax.fori_loop(1, count, step, 0, unroll=True)

    def send_parts(e, cam):
        both = jnp.dot(gather_ref[cam], cols_ref[e], preferred_element_type=f32)
        total = both[:, 0:128] + both[:, 128:256]
        part_ref[e] = total.reshape(part_ref.shape[1:])
        each(lambda d: part_copy(e, d, me).start())

    def send_ratio(e, cam):
        def take(d, total):
            source = wrapped(me + d, count)
            part_copy(e, d, source).wait_recv()
            return total + recv_ref[e, source]

        total = lax.fori_loop(1, count, take, part_ref[e, me], unroll=True)
        ratio = jnp.log(img_ref[e, cam] + 1.0) - jnp.log(total + 1.0)
        ratio = jnp.concatenate([ratio, jnp.zeros((RATIO_ROWS - PROJ_ROWS, 128), f32)], axis=0)
        ratio_ref[e, pl.ds(pl.multiple_of(me * RATIO_ROWS, RATIO_ROWS), RATIO_ROWS), :] = (
            ratio.astype(bf16)
        )
        each(lambda d: ratio_copy(e, d, me).start())

    def collect_ratio(e):
        each(lambda d: ratio_copy(e, d, wrapped(me + d, count)).wait_recv())
        each(lambda d: part_copy(e, d, me).wait_send())
        each(lambda d: ratio_copy(e, d, me).wait_send())

    def updated_rows(e, cam, rows):
        near = jnp.dot(spread_ref[cam, rows, :], ratio_ref[e], preferred_element_type=f32)
        back = by_library(near.astype(bf16), cam, rows, bwd_ref[cam])
        return vol_ref[e, rows, :] * jnp.exp(back)

    for e in range(2):
        def first(rows, _):
            vol = init_ref[e, rows, :]
            vol_ref[e, rows, :] = vol
            project_rows(e, 0, rows, vol)
            return 0

        chunks(columns, first, 2)(0)
        if e == 0:
            barrier_done()
        send_parts(e, 0)

    def round_step(r, _):
        cam = lax.rem(r, cams)
        following = lax.rem(r + 1, cams)
        for e in range(2):
            send_ratio(e, cam)
        for e in range(2):
            collect_ratio(e)

            def both(rows, _):
                vol = updated_rows(e, cam, rows)
                vol_ref[e, rows, :] = vol
                project_rows(e, following, rows, vol)
                return 0

            chunks(columns, both, 4)(0)
            send_parts(e, following)
        return 0

    lax.fori_loop(0, SWEEPS * cams - 1, round_step, 0)
    for e in range(2):
        send_ratio(e, cams - 1)
    for e in range(2):
        collect_ratio(e)

        def final(rows, carry):
            vol = updated_rows(e, cams - 1, rows)
            vol_ref[e, rows, :] = vol
            tiles = vol.reshape(CHUNK // 8, 8, 128)
            return (
                jnp.minimum(carry[0], jnp.min(tiles, axis=0)),
                jnp.maximum(carry[1], jnp.max(tiles, axis=0)),
                carry[2] + jnp.sum(tiles, axis=0),
            )

        low = jnp.full((8, 128), 3.0e38, f32)
        least, largest, total = chunks(columns, final, 2)((low, -low, jnp.zeros((8, 128), f32)))
        finish(e, whole(least, jnp.min), whole(largest, jnp.max), whole(total, jnp.sum))


def exchange(vol_ref, code_ref, high_ref, low_ref, send_own, send_on, arrive, stats):
    f32 = jnp.float32
    wide, narrow = lax.axis_size("wide"), lax.axis_size("narrow")
    me, row = lax.axis_index("wide"), lax.axis_index("narrow")
    columns = vol_ref.shape[1]
    has_wide = {-1: me > 0, 1: me < wide - 1}
    has_narrow = {-1: row > 0, 1: row < narrow - 1}

    def encode(e, least, largest):
        base = jnp.floor(jnp.log(least) * 64.0)
        extent = jnp.floor(jnp.log(largest) * 64.0) - base + 2.0
        scale = (64.0 * STEPS) / extent
        shift = base * (1.0 / 64.0)

        def step(rows, _):
            level = (jnp.log(vol_ref[e, rows, :]) - shift) * scale
            code_ref[1, 1, e, rows, :] = (
                jnp.round(level - STEPS / 2).astype(jnp.int32).astype(jnp.int16)
            )
            return 0

        chunks(columns, step, 1)(0)
        mark = jnp.where(lax.broadcasted_iota(jnp.int32, (MARK, 128), 0) < 8, base, extent)
        code_ref[1, 1, e, columns : columns + MARK, :] = mark.astype(jnp.int32).astype(jnp.int16)

    def side_copy(e, by, place):
        return pltpu.make_async_remote_copy(
            src_ref=code_ref.at[1, 1, e],
            dst_ref=code_ref.at[1 + place, 1, e],
            send_sem=send_own.at[0, (by + 1) // 2, e],
            recv_sem=arrive.at[1 + place, 1, e],
            device_id={"wide": me + by},
            device_id_type=MESH,
        )

    def row_copy(e, column, by, place):
        sem = send_own.at[1, (by + 1) // 2, e]
        if column != 0:
            sem = send_on.at[(column + 1) // 2, (by + 1) // 2, e]
        return pltpu.make_async_remote_copy(
            src_ref=code_ref.at[1 + column, 1, e],
            dst_ref=code_ref.at[1 + column, 1 + place, e],
            send_sem=sem,
            recv_sem=arrive.at[1 + column, 1 + place, e],
            device_id={"narrow": row + by},
            device_id_type=MESH,
        )

    def send(e):
        for by in (-1, 1):
            @pl.when(has_narrow[by])
            def _():
                row_copy(e, 0, by, -by).start()

            @pl.when(has_wide[by])
            def _():
                side_copy(e, by, -by).start()

    def pass_on(e):
        for side in (-1, 1):
            @pl.when(has_wide[side])
            def _():
                side_copy(e, side, side).wait_recv()
                for by in (-1, 1):
                    @pl.when(has_narrow[by])
                    def _():
                        row_copy(e, side, by, -by).start()

    def settle(e):
        for by in (-1, 1):
            @pl.when(has_narrow[by])
            def _():
                row_copy(e, 0, by, -by).wait_send()

            @pl.when(has_wide[by])
            def _():
                side_copy(e, by, -by).wait_send()
                for up in (-1, 1):
                    @pl.when(has_narrow[up])
                    def _():
                        row_copy(e, by, up, -up).wait_send()

    def place(e, i, j, values_of):
        def step(x, _):
            high, low = split(values_of(x))
            high_ref[e, (1 + i) * BRICK + x, (1 + j) * BRICK : (2 + j) * BRICK, :] = high
            low_ref[e, (1 + i) * BRICK + x, (1 + j) * BRICK : (2 + j) * BRICK, :] = low
            return 0

        lax.fori_loop(0, BRICK, step, 0, unroll=4)

    def place_own(e):
        place(e, 0, 0, lambda x: vol_ref[
            e, pl.ds(pl.multiple_of(x * BRICK, BRICK), BRICK), :] - stats[e])

    def place_code(e, i, j):
        mark = code_ref[1 + i, 1 + j, e, columns : columns + MARK, :].astype(f32)
        step = mark[8:9] * (1.0 / (64.0 * STEPS))
        shift = mark[0:1] * (1.0 / 64.0) + step * (STEPS / 2)

        def values_of(x):
            rows = pl.ds(pl.multiple_of(x * BRICK, BRICK), BRICK)
            code = code_ref[1 + i, 1 + j, e, rows, :].astype(f32)
            return jnp.exp(code * step + shift) - stats[e]

        place(e, i, j, values_of)

    def receive(e, i, j):
        here = has_narrow[j] if j else None
        if i:
            here = has_wide[i] if here is None else here & has_wide[i]

        @pl.when(here)
        def _():
            if j:
                row_copy(e, i, j, j).wait_recv()
            place_code(e, i, j)

        @pl.when(jnp.logical_not(here))
        def _():
            place(e, i, j, lambda x: jnp.zeros((BRICK, 128), f32) - stats[e])

    return encode, send, pass_on, settle, place_own, receive


def windows(place_ref, tables, high_ref, low_ref, mids, specs, corr_ref, out_ref):
    left_ref, right_ref, inv_left_ref, inv_right_ref, weight_ref = tables
    mid_high, mid_low = mids
    spec0, spec1 = specs
    f32, bf16 = jnp.float32, jnp.bfloat16
    half = DISP // 2
    wide_y = high_ref.shape[2]

    def transform(w, e, store):
        start_x, start_y, start_z = place_ref[0, w], place_ref[1, w], place_ref[2, w]
        lead = jnp.where(start_y >= 16, start_y - 16, start_y)
        later = lax.broadcasted_iota(jnp.int32, (SPAN, 128), 0) * 0 + start_y >= 16
        lane = lax.broadcasted_iota(jnp.int32, (2 * KEPT, 256), 1)
        spot = lax.rem(lane, SPAN)
        keep = (spot >= lead) & (spot < lead + WIN) & (lane < 3 * SPAN)
        left = jnp.where(keep, left_ref[...].astype(f32), 0.0).astype(bf16)
        wide = 128 * (e + 1)
        row = lax.rem(lax.broadcasted_iota(jnp.int32, (256, wide), 0), 128)
        keep = (row >= start_z) & (row < start_z + WIN)
        right_high = jnp.where(keep, right_ref[0, :, 0:wide].astype(f32), 0.0).astype(bf16)
        right_low = jnp.where(keep, right_ref[1, :, 0:wide].astype(f32), 0.0).astype(bf16)

        def turn_y(i, _):
            sides = []
            for j in range(2):
                high, low = high_ref[e, start_x + 2 * i + j], low_ref[e, start_x + 2 * i + j]
                high = jnp.where(later, high[wide_y - SPAN :], high[:SPAN])
                low = jnp.where(later, low[wide_y - SPAN :], low[:SPAN])
                sides.append(jnp.concatenate([high, low, high, high[0:16]], axis=0))
            mixed = jnp.dot(left, jnp.concatenate(sides, axis=1), preferred_element_type=f32)
            high, low = split(mixed)
            for j in range(2):
                lanes = slice(j * 128, (j + 1) * 128)
                for source, target in ((high, mid_high), (low, mid_low)):
                    target[2 * i + j, :, 0:128] = source[0:KEPT, lanes]
                    target[2 * i + j, :, 128:256] = source[KEPT : 2 * KEPT, lanes]
            return 0

        lax.fori_loop(0, WIN // 2, turn_y, 0, unroll=4)

        def turn_z(i, _):
            xs = pl.ds(i * 16, 16)
            high = mid_high[xs].reshape(16 * KEPT, 256)
            low = mid_low[xs].reshape(16 * KEPT, 256)
            value = jnp.dot(high, right_high, preferred_element_type=f32)
            value += jnp.dot(low, right_high, preferred_element_type=f32)
            value += jnp.dot(high, right_low, preferred_element_type=f32)
            store(i * 16, value.reshape(16, KEPT, wide))
            return 0

        lax.fori_loop(0, WIN // 16, turn_z, 0)

    def first(w, _):
        def store(x, value):
            spec0[w, pl.ds(x, 16)] = value

        transform(w, 0, store)
        return 0

    def second(w, _):
        def store(x, value):
            spec1[pl.ds(x + half, 16)] = value

        transform(w, 1, store)

        def sums(x, carry):
            return carry[0] + spec0[w, x, 0:8, :], carry[1] + spec1[x + half, 0:8, :]

        mean0, mean1 = lax.fori_loop(
            0, WIN, sums, (jnp.zeros((8, 128), f32), jnp.zeros((8, 256), f32)), unroll=4
        )
        lane = lax.broadcasted_iota(jnp.int32, (8, 256), 1)
        row = lax.broadcasted_iota(jnp.int32, (8, 256), 0)
        mean1 = jnp.where((row == 0) & ((lane == 0) | (lane == 192)), mean1 * (1.0 / WIN), 0.0)
        lane = lax.broadcasted_iota(jnp.int32, (8, 128), 1)
        row = lax.broadcasted_iota(jnp.int32, (8, 128), 0)
        mean0 = jnp.where((row == 0) & (lane == 0), mean0 * (1.0 / WIN), 0.0)

        def centre(x, carry):
            spec0[w, x, 0:8, :] = spec0[w, x, 0:8, :] - mean0
            spec1[x + half, 0:8, :] = spec1[x + half, 0:8, :] - mean1
            value0, value1 = spec0[w, x], spec1[x + half, :, 0:128]
            return carry[0] + value0 * value0, carry[1] + value1 * value1

        zero = jnp.zeros((KEPT, 128), f32)
        power0, power1 = lax.fori_loop(0, WIN, centre, (zero, zero), unroll=2)
        count = 1.0 / (WIN * WIN * WIN**3)
        rms0 = jnp.sqrt(whole(power0 * weight_ref[...], jnp.sum) * count + 1e-6)
        rms1 = jnp.sqrt(whole(power1 * weight_ref[...], jnp.sum) * count + 1e-6)
        spec1[0:half] = spec1[WIN : WIN + half]
        spec1[WIN + half : WIN + DISP] = spec1[half:DISP]

        def group(g, _):
            first = lax.div(g, KEPT // 8) * half
            rows = pl.ds(pl.multiple_of((g - lax.div(g, KEPT // 8) * (KEPT // 8)) * 8, 8), 8)

            def block(i, carry):
                carry = list(carry)
                base = i * 4
                ones = [spec0[w, base + j, rows, :] for j in range(4)]
                plain = [spec1[base + first + j, rows, 0:128] for j in range(half + 3)]
                swapped = [spec1[base + first + j, rows, 128:256] for j in range(half + 3)]
                for j in range(4):
                    for s in range(half):
                        carry[s] = carry[s] + ones[j] * plain[j + s]
                        carry[half + s] = carry[half + s] + ones[j] * swapped[j + s]
                return tuple(carry)

            zero = jnp.zeros((8, 128), f32)
            done = lax.fori_loop(0, WIN // 4, block, (zero,) * DISP)
            for s in range(half):
                corr_ref[first + s, rows, 0:128] = done[s]
                corr_ref[first + s, rows, 128:256] = done[half + s]
            return 0

        lax.fori_loop(0, 2 * (KEPT // 8), group, 0)

        highest = lax.Precision.HIGHEST
        turned = []
        for s in range(DISP):
            value = jnp.dot(
                inv_left_ref[...], corr_ref[s], precision=highest, preferred_element_type=f32
            )
            turned.append(jnp.concatenate([value[0:DISP], value[DISP : 2 * DISP]], axis=1))
        final = jnp.dot(
            jnp.concatenate(turned, axis=0), inv_right_ref[...],
            precision=highest, preferred_element_type=f32,
        )
        scale = 1.0 / (WIN * WIN * WIN**1.5)
        out_ref[w] = (final * (scale / (rms0 * rms1)))[:, 0:DISP]
        return 0

    return first, second


def piv_kernel(
    place_ref, init_ref, img_ref, fwd_ref, bwd_ref, lib_ref, gather_ref, spread_ref,
    left_ref, right_ref, inv_left_ref, inv_right_ref, weight_ref,
    vol_ref, out_ref,
    cols_ref, part_ref, recv_ref, ratio_ref,
    code_ref, high_ref, low_ref, mid_high, mid_low, spec0, spec1, corr_ref,
    part_send, part_recv, ratio_send, ratio_recv, send_own, send_on, arrive,
):
    count, depth = lax.axis_size("wide"), lax.axis_size("narrow")
    me, row = lax.axis_index("wide"), lax.axis_index("narrow")
    barrier = pltpu.get_barrier_semaphore()

    def greet(d, _):
        pl.semaphore_signal(
            barrier, inc=1, device_id={"wide": wrapped(me + d, count)}, device_id_type=MESH
        )
        return 0

    lax.fori_loop(1, count, greet, 0)
    for by in (1, depth - 1):
        pl.semaphore_signal(
            barrier, inc=1, device_id={"narrow": wrapped(row + by, depth)}, device_id_type=MESH
        )

    def barrier_done():
        pl.semaphore_wait(barrier, count + 1)

    stats = {}
    encode, send, pass_on, settle, place_own, receive = exchange(
        vol_ref, code_ref, high_ref, low_ref, send_own, send_on, arrive, stats
    )

    def finish(e, least, largest, total):
        stats[e] = total * (1.0 / (vol_ref.shape[1] * 128))
        encode(e, least, largest)
        send(e)

    reconstruct(
        (init_ref, img_ref, fwd_ref, bwd_ref, lib_ref, gather_ref, spread_ref, vol_ref),
        (cols_ref, part_ref, recv_ref, ratio_ref, part_send, part_recv, ratio_send, ratio_recv),
        barrier_done,
        finish,
    )
    place_own(0)
    pass_on(0)
    for i in (-1, 1):
        receive(0, i, 0)
    place_own(1)
    pass_on(1)
    for i, j in ((0, -1), (0, 1), (-1, -1), (-1, 1), (1, -1), (1, 1)):
        receive(0, i, j)
    first, second = windows(
        place_ref,
        (left_ref, right_ref, inv_left_ref, inv_right_ref, weight_ref),
        high_ref, low_ref, (mid_high, mid_low), (spec0, spec1), corr_ref, out_ref,
    )
    lax.fori_loop(0, out_ref.shape[0], first, 0)
    for i, j in ((-1, 0), (1, 0), (0, -1), (0, 1), (-1, -1), (-1, 1), (1, -1), (1, 1)):
        receive(1, i, j)
    for e in range(2):
        settle(e)
    lax.fori_loop(0, out_ref.shape[0], second, 0)


def body(initial, images, blocks, lib_index, tile_map, win_x, win_y, win_z):
    count = lax.axis_size("wide")
    own = lax.axis_index("wide")
    f32, bf16 = jnp.float32, jnp.bfloat16
    cams, members = blocks.shape[0], blocks.shape[1]
    columns = initial.shape[1] * initial.shape[2]
    tiles = images.shape[2] * images.shape[3]
    windows_count = win_x.size
    ids = tile_map.reshape(cams, columns)
    strips = own - count // 2 + ids // tiles
    inside = (strips >= 0) & (strips < count)
    gather_ids = jnp.where(inside, strips * PROJ_ROWS + ids % tiles, -1)
    spread_ids = jnp.where(inside, strips * RATIO_ROWS + ids % tiles, -1)
    gather = gather_ids[:, None, :] == lax.broadcasted_iota(
        jnp.int32, (cams, count * PROJ_ROWS, columns), 1
    )
    spread = spread_ids[:, :, None] == lax.broadcasted_iota(
        jnp.int32, (cams, columns, count * RATIO_ROWS), 2
    )
    lib = jnp.broadcast_to(lib_index.reshape(cams, columns, 1), (cams, columns, 128))
    pairs = blocks.reshape(cams, members // 2, 2, 128, 128)
    backward = pairs.transpose(0, 2, 3, 1, 4).reshape(cams, 256, members * 64)
    forward = pairs.transpose(0, 2, 4, 1, 3).reshape(cams, 256, members * 64)
    pictures = jnp.pad(
        images.reshape(2, cams, tiles, 128), ((0, 0), (0, 0), (0, PROJ_ROWS - tiles), (0, 0))
    )
    places = jnp.stack([win_x.reshape(-1), win_y.reshape(-1), win_z.reshape(-1)])
    vmem = pl.BlockSpec(memory_space=pltpu.VMEM)
    wide_x, wide_y = 3 * BRICK, 3 * BRICK
    volume, correlation = pl.pallas_call(
        piv_kernel,
        out_shape=(
            jax.ShapeDtypeStruct((2, columns, 128), f32),
            jax.ShapeDtypeStruct((windows_count, DISP * DISP, DISP), f32),
        ),
        in_specs=[pl.BlockSpec(memory_space=pltpu.SMEM)] + [vmem] * 12,
        out_specs=(vmem, vmem),
        scratch_shapes=[
            pltpu.VMEM((2, columns, 256), bf16),
            pltpu.VMEM((2, count, PROJ_ROWS, 128), f32),
            pltpu.VMEM((2, count, PROJ_ROWS, 128), f32),
            pltpu.VMEM((2, count * RATIO_ROWS, 128), bf16),
            pltpu.VMEM((3, 3, 2, columns + MARK, 128), jnp.int16),
            pltpu.VMEM((2, wide_x, wide_y, 128), bf16),
            pltpu.VMEM((2, wide_x, wide_y, 128), bf16),
            pltpu.VMEM((WIN, KEPT, 256), bf16),
            pltpu.VMEM((WIN, KEPT, 256), bf16),
            pltpu.VMEM((windows_count, WIN, KEPT, 128), f32),
            pltpu.VMEM((WIN + DISP, KEPT, 256), f32),
            pltpu.VMEM((DISP, KEPT, 256), f32),
            pltpu.SemaphoreType.DMA((2, count)),
            pltpu.SemaphoreType.DMA((2, count)),
            pltpu.SemaphoreType.DMA((2, count)),
            pltpu.SemaphoreType.DMA((2, count)),
            pltpu.SemaphoreType.DMA((2, 2, 2)),
            pltpu.SemaphoreType.DMA((2, 2, 2)),
            pltpu.SemaphoreType.DMA((3, 3, 2)),
        ],
        compiler_params=pltpu.CompilerParams(
            collective_id=0, has_side_effects=True, vmem_limit_bytes=60 * 1024 * 1024
        ),
        name="piv",
    )(
        places,
        initial.reshape(2, columns, 128),
        pictures,
        forward,
        backward,
        lib.astype(bf16),
        gather.astype(bf16),
        spread.astype(bf16),
        *[jnp.asarray(table) for table in window_tables()],
    )
    return (
        volume.reshape(initial.shape),
        correlation.reshape(1, 1, windows_count, DISP * DISP * DISP),
    )


def solution(mesh):
    placed = (
        P(None, "wide", "narrow", None),
        P(None, None, "wide", "narrow", None),
        P(),
        P(None, "wide", "narrow"),
        P(None, "wide", "narrow"),
        P("wide", "narrow", None),
        P("wide", "narrow", None),
        P("wide", "narrow", None),
    )
    return jax.shard_map(
        body,
        mesh=mesh,
        in_specs=placed,
        out_specs=(P(None, "wide", "narrow", None), P("wide", "narrow", None, None)),
        check_vma=False,
    )
```

time: 738 us -> 207 us (0.28); the launches traced: 728 us -> 206 us
  matrix products: 367 us -> 0 us
  Pallas kernels: 110 us -> 183 us
  local copies, waits for them, and re-layouts: 84.8 us -> 13.1 us
  waiting for transfers between devices: 50.3 us -> 0 us
  other arithmetic: 58.5 us -> 9.22 us
  loops' own time: 29.3 us -> 0 us
  starting transfers between devices: 26.9 us -> 0 us
    dot_general x76 -> x0, matrix products: 367 us -> none  [the longest x16 135 us: turn_axis(): real_cos = jnp.einsum(form, real_part, cosine, precision=highest)]
    pallas_call x1, Pallas kernels: 110 us -> 183 us  [body(): pl.pallas_call(piv_kernel, out_shape=(jax.ShapeDtypeStruct((2, columns, 1...]
    ppermute x4 -> x0, waiting for transfers between devices: 50.3 us -> none  [the longest x2 44.2 us: padded_2(): lax.ppermute(lax.slice_in_dim(block, 0, width, axis=dim), axis, backward)]
    another operation x1 -> x0, loops' own time: 29.3 us -> none  [body(): results = lax.map(per_window, starts)]
    reduce_sum x8 -> x0, other arithmetic: 28.8 us -> none  [the longest x4 14.4 us: window_correlation(): centred = window - jnp.mean(window, axis=(1, 2, 3), keepdims=True)]
    dot_general x16 -> x0, local copies, waits for them, and re-layouts: 28.4 us -> none  [the longest x4 8.69 us: turn_axis(): imag_sin = jnp.einsum(form, imag_part, sine_table, precision=highest)]
    ppermute x4 -> x0, starting transfers between devices: 26.9 us -> none  [the longest x2 21.6 us: padded_2(): lax.ppermute(lax.slice_in_dim(block, 0, width, axis=dim), axis, backward)]
    add x4 -> x0, local copies, waits for them, and re-layouts: 22.6 us -> none  [turn_axis(): return (real_cos - sign * imag_sin, imag_cos + sign * real_sin)]
  transfers between devices with their start and end apart: 4 -> 0, of which waited for: 4 -> 0; matrix products, arithmetic and copies ran while one was open for 0% -> 0% of each run, Pallas kernels for 0% -> 0%
where the time goes in v3:
time: 207 us; the launch traced here: 206 us
  Pallas kernels  183 us (88%)
  local copies, waits for them, and re-layouts  13.1 us (6%)
  other arithmetic  9.22 us (4%)
    pallas_call x1, Pallas kernels, body(): pl.pallas_call(piv_kernel, out_shape=(jax.ShapeDtypeStruct((2, columns, 1...  183 us

profile of v3, /device:TPU:9, one launch (start us, length us, event | category | flops | bytes accessed | tf_op | source)
XLA Modules:
  0.0 206.1 jit_solution(1097412391122592481)
XLA Ops:
  0.6 0.0 copy-start
  0.6 1.4 pad_add_fusion.place_ref
  2.0 0.9 sign_compare_fusion
  2.9 0.1 ne.56
  3.0 0.8 convert_element_type.13
  3.8 0.1 convert_element_type.14
  3.9 0.9 copy.18
  4.8 0.7 pad.4.img_ref
  5.5 0.9 broadcast_divide_fusion
  6.4 0.1 div.18
  6.5 0.1 rem.31
  6.6 1.7 broadcast_in_dim.5.lib_ref
  8.2 2.0 copy.22
  10.3 1.3 reshape.98.bwd_ref
  11.6 0.0 copy-done
  11.6 0.7 copy.19
  12.3 1.2 reshape.97.fwd_ref
  13.5 2.9 %fusion.1.gather_ref = bf16[4,384,1024]{2,1,0:T(8,128)(2,1)} fusion(s32[4,1024]{1,0:T(4,128)S(1)} %get-tuple-element.9), kind=kLoop, calls=%fused_computation.3 | loop fusion | flops 3145728 | bytes 3162112 | tf_op jit(solution)/shard_map/convert_element_type | solution.py:622
  16.4 2.4 %fusion.spread_ref = bf16[4,1024,512]{2,1,0:T(8,128)(2,1)} fusion(s32[4,1024]{1,0:T(4,128)S(1)} %get-tuple-element.8), kind=kLoop, calls=%fused_computation.1 | loop fusion | flops 4194304 | bytes 4210688 | tf_op jit(solution)/shard_map/convert_element_type | solution.py:623
  18.8 183.2 %piv.1 = (f32[2,1024,128]{2,1,0:T(8,128)}, f32[4,256,16]{2,1,0:T(8,128)}) custom-call(s32[3,4]{1,0:T(4,128)} %pad_add_fusion.place_ref, f32[2,1024,128]{2,1,0:T(8,128)} %bitcast.16, f32[2,4,24,128]{3,2,1,0:T(8,128)} %pad.4.img_ref, bf16[4,256,512]{2,1,0:T(8,128)(2,1)} %reshape.97.fwd_ref, bf16[4,256,512]{2,1,0:T(8,128)(2,1)} %reshape.98.bwd_ref, ...), custom_call_target="tpu_custom_call" | custom-call | tf_op jit(solution)/shard_map/piv/pallas_call | solution.py:582
  201.9 2.0 reshape.100
  203.9 2.3 %copy.24 = f32[2,32,32,128]{3,2,1,0:T(8,128)} copy(f32[2,32,32,128]{3,2,1,0:T(8,128)} %bitcast.15) | data formatting | bytes 2097152
  (1 shorter events, 0.0 us)
Async XLA Ops:
  0.6 10.9 %copy-start = (bf16[4,8,128,128]{3,2,1,0:T(8,128)(2,1)S(1)}, bf16[4,8,128,128]{3,2,1,0:T(8,128)(2,1)}, u32[]{:S(2)}) copy-start(bf16[4,8,128,128]{3,2,1,0:T(8,128)(2,1)} %param.15) | copy-start | bytes 3145732

commit v4 on v3

--- a/solution.py
+++ b/solution.py
@@ -19,6 +19,7 @@
 BRICK = 32
 MARK = 16
 STEPS = 65000.0
+TILES = 18
 
 
 def split(values):
@@ -57,9 +58,9 @@
     inverse_left[DISP:, : len(waves)] = weight * np.sin(angle)
     angle = turn * np.arange(WIN)[:, None] * shifts[None, :]
     cosine, sine = np.cos(angle), np.sin(angle)
-    inverse_right = np.zeros((512, 128))
-    inverse_right[:, :DISP] = np.concatenate(
-        [cosine, cosine, -sine, sine, -sine, -sine, -cosine, cosine]
+    inverse_right = np.tile(
+        np.concatenate([cosine, cosine, -sine, sine, -sine, -sine, -cosine, cosine]),
+        (1, 128 // DISP),
     )
     row_weight = np.zeros((KEPT, 128))
     row_weight[: len(waves)] = weight[:, None]
@@ -83,6 +84,53 @@
         return action(pl.ds(pl.multiple_of(i * CHUNK, CHUNK), CHUNK), carry)
 
     return lambda init: lax.fori_loop(0, rows // CHUNK, step, init, unroll=unroll)
+
+
+def prepare(turned_ref, blocks_ref, ids_ref, marks_ref, fwd_ref, bwd_ref, lib_ref, gather_ref, spread_ref):
+    f32, bf16 = jnp.float32, jnp.bfloat16
+    count = lax.axis_size("wide")
+    me = lax.axis_index("wide")
+    cams, members = blocks_ref.shape[0], blocks_ref.shape[1]
+    columns = lib_ref.shape[1]
+
+    def strip_rows(ids, stride):
+        slot = jnp.floor((ids + 0.5) * (1.0 / TILES))
+        owner = slot + (me - count // 2).astype(f32)
+        inside = (owner >= 0.0) & (owner < count)
+        return jnp.where(inside, owner * stride + (ids - slot * TILES), -1.0)
+
+    def camera(cam, _):
+        for m in range(members):
+            rows = slice(m % 2 * 128, m % 2 * 128 + 128)
+            lanes = slice(m // 2 * 128, m // 2 * 128 + 128)
+            fwd_ref[cam, rows, lanes] = turned_ref[cam, m]
+            bwd_ref[cam, rows, lanes] = blocks_ref[cam, m]
+        ids = strip_rows(ids_ref[cam].astype(f32), PROJ_ROWS)
+
+        def gather(i, _):
+            rows = pl.ds(pl.multiple_of(i * 32, 32), 32)
+            row = lax.broadcasted_iota(jnp.int32, (32, columns), 0) + i * 32
+            gather_ref[cam, rows, :] = jnp.where(row.astype(f32) == ids, 1.0, 0.0).astype(bf16)
+            return 0
+
+        lax.fori_loop(0, count * PROJ_ROWS // 32, gather, 0)
+
+        def spread(i, _):
+            rows = pl.ds(pl.multiple_of(i * 64, 64), 64)
+            mark = marks_ref[cam, rows, :].astype(f32)
+            lib = jnp.floor(mark * (1.0 / 512.0))
+            lib_ref[cam, rows, :] = lib.astype(bf16)
+            ids = strip_rows(mark - lib * 512.0, RATIO_ROWS)
+            lane = lax.broadcasted_iota(jnp.int32, (64, 128), 1).astype(f32)
+            for part in range(count * RATIO_ROWS // 128):
+                here = jnp.where(lane + part * 128.0 == ids, 1.0, 0.0)
+                spread_ref[cam, rows, part * 128 : (part + 1) * 128] = here.astype(bf16)
+            return 0
+
+        lax.fori_loop(0, columns // 64, spread, 0)
+        return 0
+
+    lax.fori_loop(0, cams, camera, 0)
 
 
 def reconstruct(refs, scratch, barrier_done, finish):
@@ -158,8 +206,10 @@
             return total + recv_ref[e, source]
 
         total = lax.fori_loop(1, count, take, part_ref[e, me], unroll=True)
-        ratio = jnp.log(img_ref[e, cam] + 1.0) - jnp.log(total + 1.0)
-        ratio = jnp.concatenate([ratio, jnp.zeros((RATIO_ROWS - PROJ_ROWS, 128), f32)], axis=0)
+        tiles = img_ref.shape[2] * img_ref.shape[3]
+        image = jnp.concatenate([img_ref[e, cam, i] for i in range(img_ref.shape[2])], axis=0)
+        ratio = jnp.log(image + 1.0) - jnp.log(total[0:tiles] + 1.0)
+        ratio = jnp.concatenate([ratio, jnp.zeros((RATIO_ROWS - tiles, 128), f32)], axis=0)
         ratio_ref[e, pl.ds(pl.multiple_of(me * RATIO_ROWS, RATIO_ROWS), RATIO_ROWS), :] = (
             ratio.astype(bf16)
         )
@@ -351,7 +401,7 @@
     return encode, send, pass_on, settle, place_own, receive
 
 
-def windows(place_ref, tables, high_ref, low_ref, mids, specs, corr_ref, out_ref):
+def windows(place_ref, tables, high_ref, low_ref, mids, specs, corr_ref, res_ref):
     left_ref, right_ref, inv_left_ref, inv_right_ref, weight_ref = tables
     mid_high, mid_low = mids
     spec0, spec1 = specs
@@ -360,7 +410,7 @@
     wide_y = high_ref.shape[2]
 
     def transform(w, e, store):
-        start_x, start_y, start_z = place_ref[0, w], place_ref[1, w], place_ref[2, w]
+        start_x, start_y, start_z = place_ref[0][w], place_ref[1][w], place_ref[2][w]
         lead = jnp.where(start_y >= 16, start_y - 16, start_y)
         later = lax.broadcasted_iota(jnp.int32, (SPAN, 128), 0) * 0 + start_y >= 16
         lane = lax.broadcasted_iota(jnp.int32, (2 * KEPT, 256), 1)
@@ -480,18 +530,24 @@
             precision=highest, preferred_element_type=f32,
         )
         scale = 1.0 / (WIN * WIN * WIN**1.5)
-        out_ref[w] = (final * (scale / (rms0 * rms1)))[:, 0:DISP]
+        final = (final * (scale / (rms0 * rms1))).reshape(DISP * DISP // 8, 8, 128)
+        lane = lax.broadcasted_iota(jnp.int32, final.shape, 2)
+        row = lax.broadcasted_iota(jnp.int32, final.shape, 1)
+        own = (lane >= row * DISP) & (lane < row * DISP + DISP)
+        final = jnp.sum(jnp.where(own, final, 0.0), axis=1)
+        res_ref[w] = final
         return 0
 
     return first, second
 
 
 def piv_kernel(
-    place_ref, init_ref, img_ref, fwd_ref, bwd_ref, lib_ref, gather_ref, spread_ref,
+    win_x_ref, win_y_ref, win_z_ref, init_ref, img_ref, turned_ref, blocks_ref, ids_ref, marks_ref,
     left_ref, right_ref, inv_left_ref, inv_right_ref, weight_ref,
     vol_ref, out_ref,
+    fwd_ref, bwd_ref, lib_ref, gather_ref, spread_ref,
     cols_ref, part_ref, recv_ref, ratio_ref,
-    code_ref, high_ref, low_ref, mid_high, mid_low, spec0, spec1, corr_ref,
+    code_ref, high_ref, low_ref, mid_high, mid_low, spec0, spec1, corr_ref, res_ref,
     part_send, part_recv, ratio_send, ratio_recv, send_own, send_on, arrive,
 ):
     count, depth = lax.axis_size("wide"), lax.axis_size("narrow")
@@ -513,6 +569,10 @@
     def barrier_done():
         pl.semaphore_wait(barrier, count + 1)
 
+    prepare(
+        turned_ref, blocks_ref, ids_ref, marks_ref,
+        fwd_ref, bwd_ref, lib_ref, gather_ref, spread_ref,
+    )
     stats = {}
     encode, send, pass_on, settle, place_own, receive = exchange(
         vol_ref, code_ref, high_ref, low_ref, send_own, send_on, arrive, stats
@@ -538,56 +598,44 @@
     for i, j in ((0, -1), (0, 1), (-1, -1), (-1, 1), (1, -1), (1, 1)):
         receive(0, i, j)
     first, second = windows(
-        place_ref,
+        (win_x_ref, win_y_ref, win_z_ref),
         (left_ref, right_ref, inv_left_ref, inv_right_ref, weight_ref),
-        high_ref, low_ref, (mid_high, mid_low), (spec0, spec1), corr_ref, out_ref,
-    )
-    lax.fori_loop(0, out_ref.shape[0], first, 0)
+        high_ref, low_ref, (mid_high, mid_low), (spec0, spec1), corr_ref, res_ref,
+    )
+    lax.fori_loop(0, spec0.shape[0], first, 0)
     for i, j in ((-1, 0), (1, 0), (0, -1), (0, 1), (-1, -1), (-1, 1), (1, -1), (1, 1)):
         receive(1, i, j)
     for e in range(2):
         settle(e)
-    lax.fori_loop(0, out_ref.shape[0], second, 0)
+    lax.fori_loop(0, spec0.shape[0], second, 0)
+    for w in range(out_ref.shape[0]):
+        for s in range(res_ref.shape[1]):
+            out_ref[w : w + 1, s * 128 : (s + 1) * 128] = res_ref[w, s : s + 1]
 
 
 def body(initial, images, blocks, lib_index, tile_map, win_x, win_y, win_z):
     count = lax.axis_size("wide")
-    own = lax.axis_index("wide")
     f32, bf16 = jnp.float32, jnp.bfloat16
     cams, members = blocks.shape[0], blocks.shape[1]
     columns = initial.shape[1] * initial.shape[2]
-    tiles = images.shape[2] * images.shape[3]
     windows_count = win_x.size
-    ids = tile_map.reshape(cams, columns)
-    strips = own - count // 2 + ids // tiles
-    inside = (strips >= 0) & (strips < count)
-    gather_ids = jnp.where(inside, strips * PROJ_ROWS + ids % tiles, -1)
-    spread_ids = jnp.where(inside, strips * RATIO_ROWS + ids % tiles, -1)
-    gather = gather_ids[:, None, :] == lax.broadcasted_iota(
-        jnp.int32, (cams, count * PROJ_ROWS, columns), 1
-    )
-    spread = spread_ids[:, :, None] == lax.broadcasted_iota(
-        jnp.int32, (cams, columns, count * RATIO_ROWS), 2
-    )
-    lib = jnp.broadcast_to(lib_index.reshape(cams, columns, 1), (cams, columns, 128))
-    pairs = blocks.reshape(cams, members // 2, 2, 128, 128)
-    backward = pairs.transpose(0, 2, 3, 1, 4).reshape(cams, 256, members * 64)
-    forward = pairs.transpose(0, 2, 4, 1, 3).reshape(cams, 256, members * 64)
-    pictures = jnp.pad(
-        images.reshape(2, cams, tiles, 128), ((0, 0), (0, 0), (0, PROJ_ROWS - tiles), (0, 0))
-    )
-    places = jnp.stack([win_x.reshape(-1), win_y.reshape(-1), win_z.reshape(-1)])
+    marks = (tile_map + 512 * lib_index).reshape(cams, columns, 1)
     vmem = pl.BlockSpec(memory_space=pltpu.VMEM)
     wide_x, wide_y = 3 * BRICK, 3 * BRICK
     volume, correlation = pl.pallas_call(
         piv_kernel,
         out_shape=(
             jax.ShapeDtypeStruct((2, columns, 128), f32),
-            jax.ShapeDtypeStruct((windows_count, DISP * DISP, DISP), f32),
+            jax.ShapeDtypeStruct((windows_count, DISP * DISP * DISP), f32),
         ),
-        in_specs=[pl.BlockSpec(memory_space=pltpu.SMEM)] + [vmem] * 12,
+        in_specs=[pl.BlockSpec(memory_space=pltpu.SMEM)] * 3 + [vmem] * 11,
         out_specs=(vmem, vmem),
         scratch_shapes=[
+            pltpu.VMEM((cams, 256, members * 64), bf16),
+            pltpu.VMEM((cams, 256, members * 64), bf16),
+            pltpu.VMEM((cams, columns, 128), bf16),
+            pltpu.VMEM((cams, count * PROJ_ROWS, columns), bf16),
+            pltpu.VMEM((cams, columns, count * RATIO_ROWS), bf16),
             pltpu.VMEM((2, columns, 256), bf16),
             pltpu.VMEM((2, count, PROJ_ROWS, 128), f32),
             pltpu.VMEM((2, count, PROJ_ROWS, 128), f32),
@@ -600,6 +648,7 @@
             pltpu.VMEM((windows_count, WIN, KEPT, 128), f32),
             pltpu.VMEM((WIN + DISP, KEPT, 256), f32),
             pltpu.VMEM((DISP, KEPT, 256), f32),
+            pltpu.VMEM((windows_count, DISP * DISP * DISP // 128, 128), f32),
             pltpu.SemaphoreType.DMA((2, count)),
             pltpu.SemaphoreType.DMA((2, count)),
             pltpu.SemaphoreType.DMA((2, count)),
@@ -613,14 +662,15 @@
         ),
         name="piv",
     )(
-        places,
+        win_x.reshape(-1),
+        win_y.reshape(-1),
+        win_z.reshape(-1),
         initial.reshape(2, columns, 128),
-        pictures,
-        forward,
-        backward,
-        lib.astype(bf16),
-        gather.astype(bf16),
-        spread.astype(bf16),
+        images,
+        blocks.transpose(0, 1, 3, 2),
+        blocks,
+        tile_map.reshape(cams, 1, columns),
+        jnp.broadcast_to(marks, (cams, columns, 128)),
         *[jnp.asarray(table) for table in window_tables()],
     )
     return (

time: 207 us -> 195 us (0.942)
  other arithmetic: 9.22 us -> 0.88 us
  local copies, waits for them, and re-layouts: 13.1 us -> 10.6 us
    reshape x6 -> x1, local copies, waits for them, and re-layouts: 8.1 us -> 1.54 us  [body(): tile_map.reshape(cams, 1, columns)]
    convert_element_type x3 -> x0, other arithmetic: 6.1 us -> none  [the longest x1 2.89 us: body(): gather.astype(bf16)]
    unnamed x3 -> x6, local copies, waits for them, and re-layouts: 2.27 us -> 6.72 us
where the time goes in v4:
time: 195 us; the launch traced here: 194 us
  Pallas kernels  182 us (93%)
  local copies, waits for them, and re-layouts  10.6 us (5%)
    pallas_call x1, Pallas kernels, body(): pl.pallas_call(piv_kernel, out_shape=(jax.ShapeDtypeStruct((2, columns, 1...  182 us
    unnamed x6, local copies, waits for them, and re-layouts  6.72 us

profile of v4, /device:TPU:9, one launch (start us, length us, event | category | flops | bytes accessed | tf_op | source)
XLA Modules:
  0.0 194.5 jit_solution(8296542554127340928)
XLA Ops:
  0.6 1.5 reshape.31.ids_ref
  2.2 0.9 multiply_add_fusion
  3.1 0.1 broadcast_in_dim.7
  3.1 1.5 copy.16.img_ref
  4.7 2.3 %copy.15 = bf16[4,8,128,128]{2,3,1,0:T(8,128)(2,1)} copy(bf16[4,8,128,128]{3,2,1,0:T(8,128)(2,1)} %blocks_ref.1) | data formatting | bytes 2097152 | tf_op args[2]
  6.9 2.2 %broadcast_in_dim.8.marks_ref = s32[4,1024,128]{2,1,0:T(8,128)} broadcast(s32[4,1024]{1,0:T(4,128)S(1)} %broadcast_in_dim.7), dimensions={0,1} | broadcast | bytes 2113536 | tf_op jit(solution)/shard_map/broadcast_in_dim | solution.py:673
  9.1 182.4 %piv.1 = (f32[2,1024,128]{2,1,0:T(8,128)}, f32[4,4096]{1,0:T(4,128)}) custom-call(s32[4]{0:T(128)} %bitcast.11, s32[4]{0:T(128)} %bitcast.12, s32[4]{0:T(128)} %bitcast.13, f32[2,1024,128]{2,1,0:T(8,128)} %bitcast.9, f32[2,4,3,6,128]{4,3,2,1,0:T(8,128)} %copy.16.img_ref, bf16[4,8,128,128]{3,2,1,0:T(8,128)(2,1)} %bitcast.7, ...), custom_call_target="tpu_custom_call" | custom-call | tf_op jit(solution)/shard_map/piv/pallas_call | solution.py:625
  191.6 0.0 copy-start
  191.6 2.3 %copy.19 = f32[2,32,32,128]{3,2,1,0:T(8,128)} copy(f32[2,32,32,128]{3,2,1,0:T(8,128)} %bitcast.8) | data formatting | bytes 2097152
  193.9 0.0 copy-done
  193.9 0.6 copy.20
Async XLA Ops:
  191.6 2.3 %copy-start = (f32[4,4096]{1,0:T(4,128)S(1)}, f32[4,4096]{1,0:T(4,128)}, u32[]{:S(2)}) copy-start(f32[4,4096]{1,0:T(4,128)} %get-tuple-element.5) | copy-start | bytes 196612

commit v5 on v4

--- a/solution.py
+++ b/solution.py
@@ -47,8 +47,8 @@
 
     angle = turn * (np.arange(128)[:, None] * np.arange(WIN)[None, :] % WIN)
     cosine, sine = np.cos(angle), np.sin(angle)
-    right = np.block([[cosine, -sine, -sine, cosine], [sine, cosine, cosine, sine]])
-    right_table = np.stack(parts(right))
+    right = np.block([[cosine, -sine], [sine, cosine]])
+    right_table = np.concatenate(parts(right), axis=1)
 
     shifts = np.arange(DISP) - DISP // 2
     weight = np.where(waves % (WIN // 2) == 0, 1.0, 2.0)
@@ -167,8 +167,8 @@
         return pltpu.make_async_remote_copy(
             src_ref=part_ref.at[e, target],
             dst_ref=recv_ref.at[e, owner],
-            send_sem=part_send.at[e, d],
-            recv_sem=part_recv.at[e, owner],
+            send_sem=part_send.at[e],
+            recv_sem=part_recv.at[e],
             device_id={"wide": target},
             device_id_type=MESH,
         )
@@ -180,31 +180,34 @@
         return pltpu.make_async_remote_copy(
             src_ref=strip(e, me),
             dst_ref=strip(e, owner),
-            send_sem=ratio_send.at[e, d],
-            recv_sem=ratio_recv.at[e, owner],
+            send_sem=ratio_send.at[e],
+            recv_sem=ratio_recv.at[e],
             device_id={"wide": wrapped(me + d, count)},
             device_id_type=MESH,
         )
 
-    def each(action):
-        def step(d, _):
-            action(d)
-            return 0
-
-        lax.fori_loop(1, count, step, 0, unroll=True)
+    def parts_done(e, sem):
+        slots = recv_ref.at[e, pl.ds(0, count - 1)]
+        pltpu.make_async_copy(slots, slots, sem.at[e]).wait()
+
+    def ratios_done(e, sem):
+        strips = ratio_ref.at[e, pl.ds(0, (count - 1) * RATIO_ROWS)]
+        pltpu.make_async_copy(strips, strips, sem.at[e]).wait()
+
+    far_first = sorted(range(1, count), key=lambda d: -(2 - abs(d % 4 - 2)) - (2 - abs(d // 4 - 2)))
 
     def send_parts(e, cam):
         both = jnp.dot(gather_ref[cam], cols_ref[e], preferred_element_type=f32)
         total = both[:, 0:128] + both[:, 128:256]
         part_ref[e] = total.reshape(part_ref.shape[1:])
-        each(lambda d: part_copy(e, d, me).start())
+        for d in far_first:
+            part_copy(e, d, me).start()
 
     def send_ratio(e, cam):
         def take(d, total):
-            source = wrapped(me + d, count)
-            part_copy(e, d, source).wait_recv()
-            return total + recv_ref[e, source]
-
+            return total + recv_ref[e, wrapped(me + d, count)]
+
+        parts_done(e, part_recv)
         total = lax.fori_loop(1, count, take, part_ref[e, me], unroll=True)
         tiles = img_ref.shape[2] * img_ref.shape[3]
         image = jnp.concatenate([img_ref[e, cam, i] for i in range(img_ref.shape[2])], axis=0)
@@ -213,12 +216,13 @@
         ratio_ref[e, pl.ds(pl.multiple_of(me * RATIO_ROWS, RATIO_ROWS), RATIO_ROWS), :] = (
             ratio.astype(bf16)
         )
-        each(lambda d: ratio_copy(e, d, me).start())
+        for d in far_first:
+            ratio_copy(e, d, me).start()
 
     def collect_ratio(e):
-        each(lambda d: ratio_copy(e, d, wrapped(me + d, count)).wait_recv())
-        each(lambda d: part_copy(e, d, me).wait_send())
-        each(lambda d: ratio_copy(e, d, me).wait_send())
+        ratios_done(e, ratio_recv)
+        parts_done(e, part_send)
+        ratios_done(e, ratio_send)
 
     def updated_rows(e, cam, rows):
         near = jnp.dot(spread_ref[cam, rows, :], ratio_ref[e], preferred_element_type=f32)
@@ -417,11 +421,9 @@
         spot = lax.rem(lane, SPAN)
         keep = (spot >= lead) & (spot < lead + WIN) & (lane < 3 * SPAN)
         left = jnp.where(keep, left_ref[...].astype(f32), 0.0).astype(bf16)
-        wide = 128 * (e + 1)
-        row = lax.rem(lax.broadcasted_iota(jnp.int32, (256, wide), 0), 128)
+        row = lax.rem(lax.broadcasted_iota(jnp.int32, (256, 256), 0), 128)
         keep = (row >= start_z) & (row < start_z + WIN)
-        right_high = jnp.where(keep, right_ref[0, :, 0:wide].astype(f32), 0.0).astype(bf16)
-        right_low = jnp.where(keep, right_ref[1, :, 0:wide].astype(f32), 0.0).astype(bf16)
+        right = jnp.where(keep, right_ref[...].astype(f32), 0.0).astype(bf16)
 
         def turn_y(i, _):
             sides = []
@@ -445,10 +447,12 @@
             xs = pl.ds(i * 16, 16)
             high = mid_high[xs].reshape(16 * KEPT, 256)
             low = mid_low[xs].reshape(16 * KEPT, 256)
-            value = jnp.dot(high, right_high, preferred_element_type=f32)
-            value += jnp.dot(low, right_high, preferred_element_type=f32)
-            value += jnp.dot(high, right_low, preferred_element_type=f32)
-            store(i * 16, value.reshape(16, KEPT, wide))
+            value = jnp.dot(high, right, preferred_element_type=f32)
+            rest = jnp.dot(low, right[:, 0:128], preferred_element_type=f32)
+            value = value[:, 0:128] + (value[:, 128:256] + rest)
+            if e == 1:
+                value = jnp.concatenate([value, pltpu.roll(value, WIN, 1)], axis=1)
+            store(i * 16, value.reshape(16, KEPT, 128 * (e + 1)))
             return 0
 
         lax.fori_loop(0, WIN // 16, turn_z, 0)
@@ -649,10 +653,10 @@
             pltpu.VMEM((WIN + DISP, KEPT, 256), f32),
             pltpu.VMEM((DISP, KEPT, 256), f32),
             pltpu.VMEM((windows_count, DISP * DISP * DISP // 128, 128), f32),
-            pltpu.SemaphoreType.DMA((2, count)),
-            pltpu.SemaphoreType.DMA((2, count)),
-            pltpu.SemaphoreType.DMA((2, count)),
-            pltpu.SemaphoreType.DMA((2, count)),
+            pltpu.SemaphoreType.DMA((2,)),
+            pltpu.SemaphoreType.DMA((2,)),
+            pltpu.SemaphoreType.DMA((2,)),
+            pltpu.SemaphoreType.DMA((2,)),
             pltpu.SemaphoreType.DMA((2, 2, 2)),
             pltpu.SemaphoreType.DMA((2, 2, 2)),
             pltpu.SemaphoreType.DMA((3, 3, 2)),

time: 195 us -> 190 us (0.974)
  Pallas kernels: 182 us -> 178 us
    pallas_call x1, Pallas kernels: 182 us -> 178 us  [body(): pl.pallas_call(piv_kernel, out_shape=(jax.ShapeDtypeStruct((2, columns, 1...]
where the time goes in v5:
time: 190 us
  Pallas kernels  178 us (94%)
  local copies, waits for them, and re-layouts  10.6 us (6%)
    pallas_call x1, Pallas kernels, body(): pl.pallas_call(piv_kernel, out_shape=(jax.ShapeDtypeStruct((2, columns, 1...  178 us
    unnamed x6, local copies, waits for them, and re-layouts  6.72 us

profile of v5, /device:TPU:9, one launch (start us, length us, event | category | flops | bytes accessed | tf_op | source)
XLA Modules:
  0.0 190.1 jit_solution(16182954574028694072)
XLA Ops:
  0.6 1.5 reshape.31.ids_ref
  2.2 0.9 multiply_add_fusion
  3.1 0.1 broadcast_in_dim.7
  3.1 1.5 copy.16.img_ref
  4.7 2.3 %copy.15 = bf16[4,8,128,128]{2,3,1,0:T(8,128)(2,1)} copy(bf16[4,8,128,128]{3,2,1,0:T(8,128)(2,1)} %blocks_ref.1) | data formatting | bytes 2097152 | tf_op args[2]
  6.9 2.2 %broadcast_in_dim.8.marks_ref = s32[4,1024,128]{2,1,0:T(8,128)} broadcast(s32[4,1024]{1,0:T(4,128)S(1)} %broadcast_in_dim.7), dimensions={0,1} | broadcast | bytes 2113536 | tf_op jit(solution)/shard_map/broadcast_in_dim | solution.py:677
  9.1 178.0 %piv.1 = (f32[2,1024,128]{2,1,0:T(8,128)}, f32[4,4096]{1,0:T(4,128)}) custom-call(s32[4]{0:T(128)} %bitcast.11, s32[4]{0:T(128)} %bitcast.12, s32[4]{0:T(128)} %bitcast.13, f32[2,1024,128]{2,1,0:T(8,128)} %bitcast.9, f32[2,4,3,6,128]{4,3,2,1,0:T(8,128)} %copy.16.img_ref, bf16[4,8,128,128]{3,2,1,0:T(8,128)(2,1)} %bitcast.7, ...), custom_call_target="tpu_custom_call" | custom-call | tf_op jit(solution)/shard_map/piv/pallas_call | solution.py:629
  187.1 0.0 copy-start
  187.2 2.3 %copy.19 = f32[2,32,32,128]{3,2,1,0:T(8,128)} copy(f32[2,32,32,128]{3,2,1,0:T(8,128)} %bitcast.8) | data formatting | bytes 2097152
  189.5 0.0 copy-done
  189.5 0.6 copy.20
Async XLA Ops:
  187.1 2.3 %copy-start = (f32[4,4096]{1,0:T(4,128)S(1)}, f32[4,4096]{1,0:T(4,128)}, u32[]{:S(2)}) copy-start(f32[4,4096]{1,0:T(4,128)} %get-tuple-element.5) | copy-start | bytes 196612

commit v6 on v5

--- a/solution.py
+++ b/solution.py
@@ -199,7 +199,7 @@
     def send_parts(e, cam):
         both = jnp.dot(gather_ref[cam], cols_ref[e], preferred_element_type=f32)
         total = both[:, 0:128] + both[:, 128:256]
-        part_ref[e] = total.reshape(part_ref.shape[1:])
+        part_ref[e] = total.reshape(count, PROJ_ROWS, 128)[:, 0 : part_ref.shape[2]]
         for d in far_first:
             part_copy(e, d, me).start()
 
@@ -211,7 +211,7 @@
         total = lax.fori_loop(1, count, take, part_ref[e, me], unroll=True)
         tiles = img_ref.shape[2] * img_ref.shape[3]
         image = jnp.concatenate([img_ref[e, cam, i] for i in range(img_ref.shape[2])], axis=0)
-        ratio = jnp.log(image + 1.0) - jnp.log(total[0:tiles] + 1.0)
+        ratio = jnp.log(image + 1.0) - jnp.log(total + 1.0)
         ratio = jnp.concatenate([ratio, jnp.zeros((RATIO_ROWS - tiles, 128), f32)], axis=0)
         ratio_ref[e, pl.ds(pl.multiple_of(me * RATIO_ROWS, RATIO_ROWS), RATIO_ROWS), :] = (
             ratio.astype(bf16)
@@ -328,12 +328,14 @@
             device_id_type=MESH,
         )
 
-    def send(e):
+    def send_rows(e):
         for by in (-1, 1):
             @pl.when(has_narrow[by])
             def _():
                 row_copy(e, 0, by, -by).start()
 
+    def send_sides(e):
+        for by in (-1, 1):
             @pl.when(has_wide[by])
             def _():
                 side_copy(e, by, -by).start()
@@ -402,7 +404,7 @@
         def _():
             place(e, i, j, lambda x: jnp.zeros((BRICK, 128), f32) - stats[e])
 
-    return encode, send, pass_on, settle, place_own, receive
+    return encode, send_rows, send_sides, pass_on, settle, place_own, receive
 
 
 def windows(place_ref, tables, high_ref, low_ref, mids, specs, corr_ref, res_ref):
@@ -578,14 +580,16 @@
         fwd_ref, bwd_ref, lib_ref, gather_ref, spread_ref,
     )
     stats = {}
-    encode, send, pass_on, settle, place_own, receive = exchange(
+    encode, send_rows, send_sides, pass_on, settle, place_own, receive = exchange(
         vol_ref, code_ref, high_ref, low_ref, send_own, send_on, arrive, stats
     )
 
     def finish(e, least, largest, total):
         stats[e] = total * (1.0 / (vol_ref.shape[1] * 128))
         encode(e, least, largest)
-        send(e)
+        if e == 0:
+            send_sides(e)
+        send_rows(e)
 
     reconstruct(
         (init_ref, img_ref, fwd_ref, bwd_ref, lib_ref, gather_ref, spread_ref, vol_ref),
@@ -595,11 +599,12 @@
     )
     place_own(0)
     pass_on(0)
-    for i in (-1, 1):
-        receive(0, i, 0)
+    send_sides(1)
     place_own(1)
+    for i, j in ((-1, 0), (1, 0), (0, -1), (0, 1)):
+        receive(0, i, j)
     pass_on(1)
-    for i, j in ((0, -1), (0, 1), (-1, -1), (-1, 1), (1, -1), (1, 1)):
+    for i, j in ((-1, -1), (-1, 1), (1, -1), (1, 1)):
         receive(0, i, j)
     first, second = windows(
         (win_x_ref, win_y_ref, win_z_ref),
@@ -641,8 +646,8 @@
             pltpu.VMEM((cams, count * PROJ_ROWS, columns), bf16),
             pltpu.VMEM((cams, columns, count * RATIO_ROWS), bf16),
             pltpu.VMEM((2, columns, 256), bf16),
-            pltpu.VMEM((2, count, PROJ_ROWS, 128), f32),
-            pltpu.VMEM((2, count, PROJ_ROWS, 128), f32),
+            pltpu.VMEM((2, count, TILES, 128), f32),
+            pltpu.VMEM((2, count, TILES, 128), f32),
             pltpu.VMEM((2, count * RATIO_ROWS, 128), bf16),
             pltpu.VMEM((3, 3, 2, columns + MARK, 128), jnp.int16),
             pltpu.VMEM((2, wide_x, wide_y, 128), bf16),

time: 190 us -> 187 us (0.984)
  Pallas kernels: 178 us -> 174 us
    pallas_call x1, Pallas kernels: 178 us -> 174 us  [body(): pl.pallas_call(piv_kernel, out_shape=(jax.ShapeDtypeStruct((2, columns, 1...]
where the time goes in v6:
time: 187 us; the launch traced here: 186 us
  Pallas kernels  174 us (93%)
  local copies, waits for them, and re-layouts  10.6 us (6%)
    pallas_call x1, Pallas kernels, body(): pl.pallas_call(piv_kernel, out_shape=(jax.ShapeDtypeStruct((2, columns, 1...  174 us
    unnamed x6, local copies, waits for them, and re-layouts  6.72 us

profile of v6, /device:TPU:9, one launch (start us, length us, event | category | flops | bytes accessed | tf_op | source)
XLA Modules:
  0.0 186.0 jit_solution(16288857812848143975)
XLA Ops:
  0.6 1.5 reshape.31.ids_ref
  2.2 0.9 multiply_add_fusion
  3.1 0.1 broadcast_in_dim.7
  3.1 1.5 copy.16.img_ref
  4.7 2.3 %copy.15 = bf16[4,8,128,128]{2,3,1,0:T(8,128)(2,1)} copy(bf16[4,8,128,128]{3,2,1,0:T(8,128)(2,1)} %blocks_ref.1) | data formatting | bytes 2097152 | tf_op args[2]
  6.9 2.2 %broadcast_in_dim.8.marks_ref = s32[4,1024,128]{2,1,0:T(8,128)} broadcast(s32[4,1024]{1,0:T(4,128)S(1)} %broadcast_in_dim.7), dimensions={0,1} | broadcast | bytes 2113536 | tf_op jit(solution)/shard_map/broadcast_in_dim | solution.py:682
  9.1 173.9 %piv.1 = (f32[2,1024,128]{2,1,0:T(8,128)}, f32[4,4096]{1,0:T(4,128)}) custom-call(s32[4]{0:T(128)} %bitcast.11, s32[4]{0:T(128)} %bitcast.12, s32[4]{0:T(128)} %bitcast.13, f32[2,1024,128]{2,1,0:T(8,128)} %bitcast.9, f32[2,4,3,6,128]{4,3,2,1,0:T(8,128)} %copy.16.img_ref, bf16[4,8,128,128]{3,2,1,0:T(8,128)(2,1)} %bitcast.7, ...), custom_call_target="tpu_custom_call" | custom-call | tf_op jit(solution)/shard_map/piv/pallas_call | solution.py:634
  183.1 0.0 copy-start
  183.1 2.3 %copy.19 = f32[2,32,32,128]{3,2,1,0:T(8,128)} copy(f32[2,32,32,128]{3,2,1,0:T(8,128)} %bitcast.8) | data formatting | bytes 2097152
  185.4 0.0 copy-done
  185.4 0.6 copy.20
Async XLA Ops:
  183.1 2.3 %copy-start = (f32[4,4096]{1,0:T(4,128)S(1)}, f32[4,4096]{1,0:T(4,128)}, u32[]{:S(2)}) copy-start(f32[4,4096]{1,0:T(4,128)} %get-tuple-element.5) | copy-start | bytes 196612

commit v7 on v6

--- a/solution.py
+++ b/solution.py
@@ -58,10 +58,16 @@
     inverse_left[DISP:, : len(waves)] = weight * np.sin(angle)
     angle = turn * np.arange(WIN)[:, None] * shifts[None, :]
     cosine, sine = np.cos(angle), np.sin(angle)
-    inverse_right = np.tile(
-        np.concatenate([cosine, cosine, -sine, sine, -sine, -sine, -cosine, cosine]),
-        (1, 128 // DISP),
-    )
+    inverse_right = np.stack([
+        np.tile(
+            np.concatenate([
+                cosine + sine, cosine - sine, even * -sine, odd * -sine,
+                cosine - sine, -sine - cosine, even * -cosine, odd * -cosine,
+            ]) + 0.0,
+            (1, 128 // DISP),
+        )
+        for even, odd in ((1, 0), (0, 1))
+    ])
     row_weight = np.zeros((KEPT, 128))
     row_weight[: len(waves)] = weight[:, None]
     f32 = np.float32
@@ -86,7 +92,9 @@
     return lambda init: lax.fori_loop(0, rows // CHUNK, step, init, unroll=unroll)
 
 
-def prepare(turned_ref, blocks_ref, ids_ref, marks_ref, fwd_ref, bwd_ref, lib_ref, gather_ref, spread_ref):
+def prepare(
+    turned_ref, blocks_ref, ids_ref, marks_ref, fwd_ref, bwd_ref, lib_ref, gather_ref, spread_ref
+):
     f32, bf16 = jnp.float32, jnp.bfloat16
     count = lax.axis_size("wide")
     me = lax.axis_index("wide")
@@ -99,13 +107,14 @@
         inside = (owner >= 0.0) & (owner < count)
         return jnp.where(inside, owner * stride + (ids - slot * TILES), -1.0)
 
-    def camera(cam, _):
+    def camera(cam):
         for m in range(members):
             rows = slice(m % 2 * 128, m % 2 * 128 + 128)
             lanes = slice(m // 2 * 128, m // 2 * 128 + 128)
             fwd_ref[cam, rows, lanes] = turned_ref[cam, m]
             bwd_ref[cam, rows, lanes] = blocks_ref[cam, m]
-        ids = strip_rows(ids_ref[cam].astype(f32), PROJ_ROWS)
+        mark = ids_ref[cam : cam + 1, :].astype(f32)
+        ids = strip_rows(mark - jnp.floor(mark * (1.0 / 512.0)) * 512.0, PROJ_ROWS)
 
         def gather(i, _):
             rows = pl.ds(pl.multiple_of(i * 32, 32), 32)
@@ -128,9 +137,9 @@
             return 0
 
         lax.fori_loop(0, columns // 64, spread, 0)
-        return 0
-
-    lax.fori_loop(0, cams, camera, 0)
+
+    for cam in range(cams):
+        camera(cam)
 
 
 def reconstruct(refs, scratch, barrier_done, finish):
@@ -452,9 +461,14 @@
             value = jnp.dot(high, right, preferred_element_type=f32)
             rest = jnp.dot(low, right[:, 0:128], preferred_element_type=f32)
             value = value[:, 0:128] + (value[:, 128:256] + rest)
-            if e == 1:
-                value = jnp.concatenate([value, pltpu.roll(value, WIN, 1)], axis=1)
-            store(i * 16, value.reshape(16, KEPT, 128 * (e + 1)))
+            other = pltpu.roll(value, WIN, 1)
+            if e == 0:
+                lane = lax.broadcasted_iota(jnp.int32, value.shape, 1)
+                other = jnp.where(lane < WIN, value - other, other - value)
+            else:
+                other = value + other
+            value = jnp.concatenate([value, other], axis=1)
+            store(i * 16, value.reshape(16, KEPT, 256))
             return 0
 
         lax.fori_loop(0, WIN // 16, turn_z, 0)
@@ -476,19 +490,18 @@
             return carry[0] + spec0[w, x, 0:8, :], carry[1] + spec1[x + half, 0:8, :]
 
         mean0, mean1 = lax.fori_loop(
-            0, WIN, sums, (jnp.zeros((8, 128), f32), jnp.zeros((8, 256), f32)), unroll=4
+            0, WIN, sums, (jnp.zeros((8, 256), f32), jnp.zeros((8, 256), f32)), unroll=4
         )
         lane = lax.broadcasted_iota(jnp.int32, (8, 256), 1)
         row = lax.broadcasted_iota(jnp.int32, (8, 256), 0)
-        mean1 = jnp.where((row == 0) & ((lane == 0) | (lane == 192)), mean1 * (1.0 / WIN), 0.0)
-        lane = lax.broadcasted_iota(jnp.int32, (8, 128), 1)
-        row = lax.broadcasted_iota(jnp.int32, (8, 128), 0)
-        mean0 = jnp.where((row == 0) & (lane == 0), mean0 * (1.0 / WIN), 0.0)
+        still = (row == 0) & ((lane == 0) | (lane == 128) | (lane == 192))
+        mean0 = jnp.where(still, mean0 * (1.0 / WIN), 0.0)
+        mean1 = jnp.where(still, mean1 * (1.0 / WIN), 0.0)
 
         def centre(x, carry):
             spec0[w, x, 0:8, :] = spec0[w, x, 0:8, :] - mean0
             spec1[x + half, 0:8, :] = spec1[x + half, 0:8, :] - mean1
-            value0, value1 = spec0[w, x], spec1[x + half, :, 0:128]
+            value0, value1 = spec0[w, x, :, 0:128], spec1[x + half, :, 0:128]
             return carry[0] + value0 * value0, carry[1] + value1 * value1
 
         zero = jnp.zeros((KEPT, 128), f32)
@@ -498,6 +511,13 @@
         rms1 = jnp.sqrt(whole(power1 * weight_ref[...], jnp.sum) * count + 1e-6)
         spec1[0:half] = spec1[WIN : WIN + half]
         spec1[WIN + half : WIN + DISP] = spec1[half:DISP]
+        lower = lax.broadcasted_iota(jnp.int32, (KEPT, 128), 1) < WIN
+
+        def pair(x, _):
+            spec1[x, :, 128:256] = jnp.where(lower, spec1[x, :, 128:256], spec1[x + 1, :, 128:256])
+            return 0
+
+        lax.fori_loop(0, WIN + DISP - 2, pair, 0, unroll=2)
 
         def group(g, _):
             first = lax.div(g, KEPT // 8) * half
@@ -506,20 +526,22 @@
             def block(i, carry):
                 carry = list(carry)
                 base = i * 4
-                ones = [spec0[w, base + j, rows, :] for j in range(4)]
+                ones = [spec0[w, base + j, rows, 0:128] for j in range(4)]
+                sums = [spec0[w, base + j, rows, 128:256] for j in range(4)]
                 plain = [spec1[base + first + j, rows, 0:128] for j in range(half + 3)]
-                swapped = [spec1[base + first + j, rows, 128:256] for j in range(half + 3)]
+                paired = [spec1[base + first + j, rows, 128:256] for j in range(half + 2)]
                 for j in range(4):
                     for s in range(half):
                         carry[s] = carry[s] + ones[j] * plain[j + s]
-                        carry[half + s] = carry[half + s] + ones[j] * swapped[j + s]
+                    for s in range(0, half, 2):
+                        carry[half + s // 2] = carry[half + s // 2] + sums[j] * paired[j + s]
                 return tuple(carry)
 
             zero = jnp.zeros((8, 128), f32)
-            done = lax.fori_loop(0, WIN // 4, block, (zero,) * DISP)
+            done = lax.fori_loop(0, WIN // 4, block, (zero,) * (half + half // 2))
             for s in range(half):
                 corr_ref[first + s, rows, 0:128] = done[s]
-                corr_ref[first + s, rows, 128:256] = done[half + s]
+                corr_ref[first + s, rows, 128:256] = done[half + s // 2]
             return 0
 
         lax.fori_loop(0, 2 * (KEPT // 8), group, 0)
@@ -531,9 +553,15 @@
                 inv_left_ref[...], corr_ref[s], precision=highest, preferred_element_type=f32
             )
             turned.append(jnp.concatenate([value[0:DISP], value[DISP : 2 * DISP]], axis=1))
-        final = jnp.dot(
-            jnp.concatenate(turned, axis=0), inv_right_ref[...],
-            precision=highest, preferred_element_type=f32,
+        sides = [
+            jnp.dot(
+                jnp.concatenate(turned[side::2], axis=0), inv_right_ref[side],
+                precision=highest, preferred_element_type=f32,
+            )
+            for side in range(2)
+        ]
+        final = jnp.concatenate(
+            [sides[s % 2][s // 2 * DISP : (s // 2 + 1) * DISP] for s in range(DISP)], axis=0
         )
         scale = 1.0 / (WIN * WIN * WIN**1.5)
         final = (final * (scale / (rms0 * rms1))).reshape(DISP * DISP // 8, 8, 128)
@@ -628,7 +656,7 @@
     cams, members = blocks.shape[0], blocks.shape[1]
     columns = initial.shape[1] * initial.shape[2]
     windows_count = win_x.size
-    marks = (tile_map + 512 * lib_index).reshape(cams, columns, 1)
+    marks = (tile_map + 512 * lib_index).reshape(cams, columns)
     vmem = pl.BlockSpec(memory_space=pltpu.VMEM)
     wide_x, wide_y = 3 * BRICK, 3 * BRICK
     volume, correlation = pl.pallas_call(
@@ -654,7 +682,7 @@
             pltpu.VMEM((2, wide_x, wide_y, 128), bf16),
             pltpu.VMEM((WIN, KEPT, 256), bf16),
             pltpu.VMEM((WIN, KEPT, 256), bf16),
-            pltpu.VMEM((windows_count, WIN, KEPT, 128), f32),
+            pltpu.VMEM((windows_count, WIN, KEPT, 256), f32),
             pltpu.VMEM((WIN + DISP, KEPT, 256), f32),
             pltpu.VMEM((DISP, KEPT, 256), f32),
             pltpu.VMEM((windows_count, DISP * DISP * DISP // 128, 128), f32),
@@ -678,8 +706,8 @@
         images,
         blocks.transpose(0, 1, 3, 2),
         blocks,
-        tile_map.reshape(cams, 1, columns),
-        jnp.broadcast_to(marks, (cams, columns, 128)),
+        marks,
+        jnp.broadcast_to(marks[:, :, None], (cams, columns, 128)),
         *[jnp.asarray(table) for table in window_tables()],
     )
     return (

time: 187 us -> 185 us (0.989)
    unnamed x6 -> x8, local copies, waits for them, and re-layouts: 6.72 us -> 6.73 us
where the time goes in v7:
time: 185 us; the launch traced here: 184 us
  Pallas kernels  173 us (94%)
  local copies, waits for them, and re-layouts  9.02 us (5%)
    pallas_call x1, Pallas kernels, body(): pl.pallas_call(piv_kernel, out_shape=(jax.ShapeDtypeStruct((2, columns, 1...  173 us
    unnamed x8, local copies, waits for them, and re-layouts  6.73 us

profile of v7, /device:TPU:9, one launch (start us, length us, event | category | flops | bytes accessed | tf_op | source)
XLA Modules:
  0.0 184.0 jit_solution(13693557766407072622)
XLA Ops:
  0.6 0.9 multiply_add_fusion
  1.5 0.1 reshape.30.ids_ref
  1.6 0.0 copy-start
  1.6 1.5 copy.16.img_ref
  3.2 2.3 %copy.15 = bf16[4,8,128,128]{2,3,1,0:T(8,128)(2,1)} copy(bf16[4,8,128,128]{3,2,1,0:T(8,128)(2,1)} %blocks_ref.1) | data formatting | bytes 2097152 | tf_op args[2]
  5.4 2.2 %broadcast_in_dim.2.marks_ref = s32[4,1024,128]{2,1,0:T(8,128)} broadcast(s32[4,1024]{1,0:T(4,128)S(1)} %reshape.30.ids_ref), dimensions={0,1} | broadcast | bytes 2113536 | tf_op jit(solution)/shard_map/broadcast_in_dim | solution.py:710
  7.6 0.0 copy-done
  7.6 173.4 %piv.1 = (f32[2,1024,128]{2,1,0:T(8,128)}, f32[4,4096]{1,0:T(4,128)}) custom-call(s32[4]{0:T(128)} %bitcast.11, s32[4]{0:T(128)} %bitcast.12, s32[4]{0:T(128)} %bitcast.13, f32[2,1024,128]{2,1,0:T(8,128)} %bitcast.9, f32[2,4,3,6,128]{4,3,2,1,0:T(8,128)} %copy.16.img_ref, bf16[4,8,128,128]{3,2,1,0:T(8,128)(2,1)} %bitcast.7, ...), custom_call_target="tpu_custom_call" | custom-call | tf_op jit(solution)/shard_map/piv/pallas_call | solution.py:662
  181.1 0.0 copy-start.1
  181.1 2.3 %copy.19 = f32[2,32,32,128]{3,2,1,0:T(8,128)} copy(f32[2,32,32,128]{3,2,1,0:T(8,128)} %bitcast.8) | data formatting | bytes 2097152
  183.4 0.0 copy-done.1
  183.4 0.6 copy.20
Async XLA Ops:
  1.6 6.0 %copy-start = (s32[4,1024]{1,0:T(4,128)}, s32[4,1024]{1,0:T(4,128)S(1)}, u32[]{:S(2)}) copy-start(s32[4,1024]{1,0:T(4,128)S(1)} %reshape.30.ids_ref) | copy-start | bytes 49156
  181.1 2.3 %copy-start.1 = (f32[4,4096]{1,0:T(4,128)S(1)}, f32[4,4096]{1,0:T(4,128)}, u32[]{:S(2)}) copy-start(f32[4,4096]{1,0:T(4,128)} %get-tuple-element.5) | copy-start | bytes 196612

commit v8 on v7

--- a/solution.py
+++ b/solution.py
@@ -93,7 +93,8 @@
 
 
 def prepare(
-    turned_ref, blocks_ref, ids_ref, marks_ref, fwd_ref, bwd_ref, lib_ref, gather_ref, spread_ref
+    img_ref, blocks_ref, ids_ref, marks_ref, logs_ref, fwd_ref, bwd_ref, lib_ref, gather_ref,
+    spread_ref,
 ):
     f32, bf16 = jnp.float32, jnp.bfloat16
     count = lax.axis_size("wide")
@@ -111,7 +112,7 @@
         for m in range(members):
             rows = slice(m % 2 * 128, m % 2 * 128 + 128)
             lanes = slice(m // 2 * 128, m // 2 * 128 + 128)
-            fwd_ref[cam, rows, lanes] = turned_ref[cam, m]
+            fwd_ref[cam, rows, lanes] = blocks_ref[cam, m].astype(f32).T.astype(bf16)
             bwd_ref[cam, rows, lanes] = blocks_ref[cam, m]
         mark = ids_ref[cam : cam + 1, :].astype(f32)
         ids = strip_rows(mark - jnp.floor(mark * (1.0 / 512.0)) * 512.0, PROJ_ROWS)
@@ -138,12 +139,26 @@
 
         lax.fori_loop(0, columns // 64, spread, 0)
 
-    for cam in range(cams):
-        camera(cam)
-
-
-def reconstruct(refs, scratch, barrier_done, finish):
-    init_ref, img_ref, fwd_ref, bwd_ref, lib_ref, gather_ref, spread_ref, vol_ref = refs
+    def pictures():
+        for e in range(2):
+            for i in range(img_ref.shape[1]):
+                for j in range(img_ref.shape[2]):
+                    tile = jnp.log(img_ref[e, i, j] + 1.0)
+                    at = i * img_ref.shape[2] + j
+                    for cam in range(cams):
+                        logs_ref[e, cam, at : at + 1, :] = tile[cam : cam + 1]
+
+    def rest():
+        pictures()
+        for cam in range(1, cams):
+            camera(cam)
+
+    camera(0)
+    return rest
+
+
+def reconstruct(refs, scratch, barrier_done, meanwhile, finish):
+    init_ref, logs_ref, fwd_ref, bwd_ref, lib_ref, gather_ref, spread_ref, vol_ref = refs
     cols_ref, part_ref, recv_ref, ratio_ref = scratch[:4]
     part_send, part_recv, ratio_send, ratio_recv = scratch[4:]
     f32, bf16 = jnp.float32, jnp.bfloat16
@@ -218,9 +233,8 @@
 
         parts_done(e, part_recv)
         total = lax.fori_loop(1, count, take, part_ref[e, me], unroll=True)
-        tiles = img_ref.shape[2] * img_ref.shape[3]
-        image = jnp.concatenate([img_ref[e, cam, i] for i in range(img_ref.shape[2])], axis=0)
-        ratio = jnp.log(image + 1.0) - jnp.log(total + 1.0)
+        tiles = logs_ref.shape[2]
+        ratio = logs_ref[e, cam] - jnp.log(total + 1.0)
         ratio = jnp.concatenate([ratio, jnp.zeros((RATIO_ROWS - tiles, 128), f32)], axis=0)
         ratio_ref[e, pl.ds(pl.multiple_of(me * RATIO_ROWS, RATIO_ROWS), RATIO_ROWS), :] = (
             ratio.astype(bf16)
@@ -249,6 +263,8 @@
         if e == 0:
             barrier_done()
         send_parts(e, 0)
+
+    meanwhile()
 
     def round_step(r, _):
         cam = lax.rem(r, cams)
@@ -576,10 +592,10 @@
 
 
 def piv_kernel(
-    win_x_ref, win_y_ref, win_z_ref, init_ref, img_ref, turned_ref, blocks_ref, ids_ref, marks_ref,
+    win_x_ref, win_y_ref, win_z_ref, init_ref, img_ref, blocks_ref, ids_ref, marks_ref,
     left_ref, right_ref, inv_left_ref, inv_right_ref, weight_ref,
     vol_ref, out_ref,
-    fwd_ref, bwd_ref, lib_ref, gather_ref, spread_ref,
+    logs_ref, fwd_ref, bwd_ref, lib_ref, gather_ref, spread_ref,
     cols_ref, part_ref, recv_ref, ratio_ref,
     code_ref, high_ref, low_ref, mid_high, mid_low, spec0, spec1, corr_ref, res_ref,
     part_send, part_recv, ratio_send, ratio_recv, send_own, send_on, arrive,
@@ -603,9 +619,9 @@
     def barrier_done():
         pl.semaphore_wait(barrier, count + 1)
 
-    prepare(
-        turned_ref, blocks_ref, ids_ref, marks_ref,
-        fwd_ref, bwd_ref, lib_ref, gather_ref, spread_ref,
+    rest = prepare(
+        img_ref, blocks_ref, ids_ref, marks_ref,
+        logs_ref, fwd_ref, bwd_ref, lib_ref, gather_ref, spread_ref,
     )
     stats = {}
     encode, send_rows, send_sides, pass_on, settle, place_own, receive = exchange(
@@ -620,9 +636,10 @@
         send_rows(e)
 
     reconstruct(
-        (init_ref, img_ref, fwd_ref, bwd_ref, lib_ref, gather_ref, spread_ref, vol_ref),
+        (init_ref, logs_ref, fwd_ref, bwd_ref, lib_ref, gather_ref, spread_ref, vol_ref),
         (cols_ref, part_ref, recv_ref, ratio_ref, part_send, part_recv, ratio_send, ratio_recv),
         barrier_done,
+        rest,
         finish,
     )
     place_own(0)
@@ -665,9 +682,10 @@
             jax.ShapeDtypeStruct((2, columns, 128), f32),
             jax.ShapeDtypeStruct((windows_count, DISP * DISP * DISP), f32),
         ),
-        in_specs=[pl.BlockSpec(memory_space=pltpu.SMEM)] * 3 + [vmem] * 11,
+        in_specs=[pl.BlockSpec(memory_space=pltpu.SMEM)] * 3 + [vmem] * 10,
         out_specs=(vmem, vmem),
         scratch_shapes=[
+            pltpu.VMEM((2, cams, TILES, 128), f32),
             pltpu.VMEM((cams, 256, members * 64), bf16),
             pltpu.VMEM((cams, 256, members * 64), bf16),
             pltpu.VMEM((cams, columns, 128), bf16),
@@ -703,8 +721,7 @@
         win_y.reshape(-1),
         win_z.reshape(-1),
         initial.reshape(2, columns, 128),
-        images,
-        blocks.transpose(0, 1, 3, 2),
+        images.transpose(0, 2, 3, 1, 4),
         blocks,
         marks,
         jnp.broadcast_to(marks[:, :, None], (cams, columns, 128)),

time: 185 us -> 179 us (0.968)
  local copies, waits for them, and re-layouts: 9.02 us -> 5.24 us
    unnamed x8 -> x6, local copies, waits for them, and re-layouts: 6.73 us -> 2.93 us
where the time goes in v8:
time: 179 us; the launch traced here: 178 us
  Pallas kernels  172 us (96%)
  local copies, waits for them, and re-layouts  5.24 us (3%)
    pallas_call x1, Pallas kernels, body(): pl.pallas_call(piv_kernel, out_shape=(jax.ShapeDtypeStruct((2, columns, 1...  172 us

profile of v8, /device:TPU:9, one launch (start us, length us, event | category | flops | bytes accessed | tf_op | source)
XLA Modules:
  0.0 178.5 jit_solution(15619020092213206586)
XLA Ops:
  0.6 0.9 multiply_add_fusion
  1.5 0.1 reshape.30.ids_ref
  1.6 0.0 copy-start
  1.6 2.2 %broadcast_in_dim.2.marks_ref = s32[4,1024,128]{2,1,0:T(8,128)} broadcast(s32[4,1024]{1,0:T(4,128)S(1)} %reshape.30.ids_ref), dimensions={0,1} | broadcast | bytes 2113536 | tf_op jit(solution)/shard_map/broadcast_in_dim | solution.py:727
  3.8 0.0 copy-done
  3.8 171.7 %piv.1 = (f32[2,1024,128]{2,1,0:T(8,128)}, f32[4,4096]{1,0:T(4,128)}) custom-call(s32[4]{0:T(128)} %bitcast.11, s32[4]{0:T(128)} %bitcast.12, s32[4]{0:T(128)} %bitcast.13, f32[2,1024,128]{2,1,0:T(8,128)} %bitcast.7, f32[2,3,6,4,128]{4,3,2,1,0:T(4,128)} %bitcast.9, bf16[4,8,128,128]{3,2,1,0:T(8,128)(2,1)} %blocks_ref.1, s32[4,1024]{1,0:T(4,128)} %copy-done, ...), custom_call_target="tpu_custom_call" | custom-call | tf_op jit(solution)/shard_map/piv/pallas_call | solution.py:679
  175.5 0.0 copy-start.1
  175.5 2.3 %copy.17 = f32[2,32,32,128]{3,2,1,0:T(8,128)} copy(f32[2,32,32,128]{3,2,1,0:T(8,128)} %bitcast.8) | data formatting | bytes 2097152
  177.8 0.0 copy-done.1
  177.8 0.6 copy.18
Async XLA Ops:
  1.6 2.2 %copy-start = (s32[4,1024]{1,0:T(4,128)}, s32[4,1024]{1,0:T(4,128)S(1)}, u32[]{:S(2)}) copy-start(s32[4,1024]{1,0:T(4,128)S(1)} %reshape.30.ids_ref) | copy-start | bytes 49156
  175.5 2.3 %copy-start.1 = (f32[4,4096]{1,0:T(4,128)S(1)}, f32[4,4096]{1,0:T(4,128)}, u32[]{:S(2)}) copy-start(f32[4,4096]{1,0:T(4,128)} %get-tuple-element.5) | copy-start | bytes 196612
